TPU v7x, 512 devices: a whole 4x4x16 slice. The times are simulated.
512 devices in a mesh: grp: 64 (over y, x, z_hi), tp: 8 (over z_lo, core).
Axes of the slice: x: 4, y: 4, z: 16 (z_hi: 4, z_lo: 4; z = z_hi * 4 + z_lo), core: 2. Of those that a mesh axis runs over, the one named last changes fastest.
Arguments:
- tokens: bfloat16 [32768, 6144], P('grp', 'tp'), may hold values from -60 to 60
- gain: float32 [6144], P('tp'), may hold values from 0.1 to 1.9
- kv_weight: bfloat16 [6144, 2048], P('tp'), may hold values from -0.078125 to 0.078125
- kv_bias: float32 [2048], P('tp'), may hold values from -3 to 3
- lengths: int32 [64, 64], replicated, may hold values from 1 to 16, 512 in all within a row
- dest: int32 [64, 64], replicated, may hold values from 0 to 63, each once within a row
- queries: bfloat16 [64, 64, 2, 8192], P('grp', None, None, 'tp'), may hold values from -16 to 16
- old_cache: bfloat16 [64, 64, 16, 2048], P('grp', None, None, 'tp'), may hold values from -4 to 4
- new_kv: bfloat16 [64, 64, 2, 2048], P('grp', None, None, 'tp'), may hold values from -5 to 5
Outputs:
- attended: bfloat16 [64, 64, 2, 8192], P('grp', None, None, 'tp')
Inputs may be any that keep to these rules, and one draw needn't show every extreme that they name: `lengths`: row g lists the prompt rows of prefill group g's requests in block order; each row sums to 512 and its largest entry is exactly 16. `dest`: each row is a permutation of the decode groups, so each decode group receives exactly one request from every prefill group.
All inputs are finite; a program needn't handle non-finite values.
Results may differ from a plain program's by a relative error of at most 0.0058.
Values may be sent and summed in bfloat16 or wider, within the bound.
A program may use at most 64 MiB of HBM per device.

v0:
```python
import math

import jax
import jax.numpy as jnp
from jax import lax
from jax.sharding import PartitionSpec as P

D = 6144
HD = 128
SLOT = 16
CACHED = 16
STEPS = 2
KVW = 2048
QPK = 8


EPSILON = 1e-06
THETA = 1000000.0


def shards(tokens, gain, kv_weight, kv_bias, lengths, dest, queries, old_cache, new_kv):
    own_group = lax.axis_index("grp")
    span_rows = tokens.shape[0]
    requests = lengths.shape[1]
    sources = dest.shape[0]
    floats = tokens.astype(jnp.float32)
    squares = jnp.sum(floats * floats, axis=1)
    totals = lax.psum(squares, "tp")
    inv_rms = lax.rsqrt(totals / D + EPSILON)
    normed = (floats * inv_rms[:, None] * gain[None, :]).astype(jnp.bfloat16)
    local_width = KVW // lax.axis_size("tp")
    head_weight = lax.all_to_all(kv_weight, "tp", split_axis=1, concat_axis=0, tiled=True)
    projected = lax.dot_general(
        head_weight,
        lax.all_gather(normed, "tp", axis=1, tiled=True),
        (((0,), (1,)), ((), ())),
        preferred_element_type=jnp.float32,
    )
    heads_here = local_width // (2 * HD)
    projected = projected + kv_bias[:, None]
    parted = projected.reshape(heads_here, 2, HD, span_rows)
    span_lengths = lengths[own_group]
    row_ends = jnp.cumsum(span_lengths)
    starts = row_ends - span_lengths
    row_index = jnp.arange(span_rows, dtype=jnp.int32)
    owning = jnp.sum((row_ends[None, :] <= row_index[:, None]).astype(jnp.int32), axis=1)
    request_ids = jnp.arange(requests, dtype=jnp.int32)
    first_row = jnp.sum(
        jnp.where(owning[:, None] == request_ids[None, :], starts[None, :], 0), axis=1
    )
    positions = (CACHED + row_index - first_row).astype(jnp.float32)
    half_width = HD // 2
    frequency = THETA ** (-2.0 * jnp.arange(half_width, dtype=jnp.float32) / HD)
    angles = positions[None, :] * frequency[:, None]
    cosine = jnp.cos(angles)
    sine_part = jnp.sin(angles)
    keys_in = parted[:, 0]
    first_half = keys_in[:, :half_width]
    second_half = keys_in[:, half_width:]
    rotated = jnp.concatenate(
        [
            first_half * cosine - second_half * sine_part,
            second_half * cosine + first_half * sine_part,
        ],
        axis=1,
    )
    key_values = (
        jnp.stack([rotated, parted[:, 1]], axis=1)
        .reshape(local_width, span_rows)
        .astype(jnp.bfloat16)
    )
    slot_ids = jnp.arange(sources, dtype=jnp.int32)
    routed = dest[own_group][None, :] == slot_ids[:, None]
    slot_first = jnp.sum(jnp.where(routed, starts[None, :], 0), axis=1)
    slot_length = jnp.sum(jnp.where(routed, span_lengths[None, :], 0), axis=1)
    slot_offsets = jnp.arange(SLOT, dtype=jnp.int32)
    picked_rows = jnp.minimum(slot_first[:, None] + slot_offsets[None, :], span_rows - 1).reshape(
        -1
    )
    slot_valid = (slot_offsets[None, :] < slot_length[:, None]).reshape(-1)
    outgoing = jnp.where(
        slot_valid[None, :], jnp.take(key_values, picked_rows, axis=1), jnp.zeros((), jnp.bfloat16)
    )
    arrived = lax.all_to_all(outgoing, "grp", split_axis=1, concat_axis=1, tiled=True)
    toward_me = dest == own_group
    live_rows = jnp.sum(jnp.where(toward_me, lengths, 0), axis=1)
    query_block = queries[0].reshape(sources, STEPS, heads_here, QPK, HD)
    old_rows = old_cache[0].reshape(sources, CACHED, heads_here, 2, HD)
    new_rows = new_kv[0].reshape(sources, STEPS, heads_here, 2, HD)
    span_kv = arrived.reshape(heads_here, 2, HD, sources, SLOT)
    score_root = math.sqrt(HD)
    score_old = (
        jnp.einsum(
            "sthgd,srhd->sthgr",
            query_block,
            old_rows[:, :, :, 0],
            preferred_element_type=jnp.float32,
        )
        / score_root
    )
    score_span = (
        jnp.einsum(
            "sthgd,hdsl->sthgl", query_block, span_kv[:, 0], preferred_element_type=jnp.float32
        )
        / score_root
    )
    score_new = (
        jnp.einsum(
            "sthgd,srhd->sthgr",
            query_block,
            new_rows[:, :, :, 0],
            preferred_element_type=jnp.float32,
        )
        / score_root
    )
    span_mask = slot_offsets[None, :] < live_rows[:, None]
    score_span = jnp.where(span_mask[:, None, None, None, :], score_span, -1e30)
    step_ids = jnp.arange(STEPS, dtype=jnp.int32)
    causal = step_ids[None, :] <= step_ids[:, None]
    score_new = jnp.where(causal[None, :, None, None, :], score_new, -1e30)
    scores = jnp.concatenate([score_old, score_span, score_new], axis=-1)
    row_max = jnp.max(scores, axis=-1, keepdims=True)
    weights = jnp.exp(scores - row_max)
    probabilities = (weights / jnp.sum(weights, axis=-1, keepdims=True)).astype(jnp.bfloat16)
    prob_old = probabilities[..., :CACHED]
    prob_span = probabilities[..., CACHED : CACHED + SLOT]
    prob_new = probabilities[..., CACHED + SLOT :]
    output = jnp.einsum(
        "sthgr,srhd->sthgd", prob_old, old_rows[:, :, :, 1], preferred_element_type=jnp.float32
    )
    output = output + jnp.einsum(
        "sthgl,hdsl->sthgd", prob_span, span_kv[:, 1], preferred_element_type=jnp.float32
    )
    output = output + jnp.einsum(
        "sthgr,srhd->sthgd", prob_new, new_rows[:, :, :, 1], preferred_element_type=jnp.float32
    )
    return output.reshape(sources, STEPS, heads_here * QPK * HD).astype(jnp.bfloat16)[None]


def solution(mesh):
    return jax.shard_map(
        shards,
        mesh=mesh,
        in_specs=(
            P("grp", "tp"),
            P("tp"),
            P("tp", None),
            P("tp"),
            P(),
            P(),
            P("grp", None, None, "tp"),
            P("grp", None, None, "tp"),
            P("grp", None, None, "tp"),
        ),
        out_specs=P("grp", None, None, "tp"),
        check_vma=False,
    )
```

profile of v0, /device:TPU:32, one launch (start us, length us, event | category | flops | bytes accessed | tf_op | source)
XLA Modules:
  0.0 251.3 jit_solution(4313050616710849223)
XLA Ops:
  6.5 4.7 %copy.40 = bf16[768,2048]{0,1:T(8,128)(2,1)} copy(bf16[768,2048]{1,0:T(8,128)(2,1)} %param.11) | data formatting | bytes 6291456 | tf_op args[2]
  11.3 9.2 %all-to-all-start = ((bf16[768,8,256]{0,2,1:T(8,128)(2,1)}), bf16[768,8,256]{0,2,1:T(8,128)(2,1)S(1)}, u32[]{:S(2)}, u32[]{:S(2)}) async-start(bf16[768,8,256]{0,2,1:T(8,128)(2,1)} %bitcast.136), calls=%async_computation | async-start | bytes 6291456 | tf_op jit(solution)/shard_map/all_to_all | solution.py:32
  20.5 1.4 fusion
  21.9 73.8 %psum.7 = f32[512]{0:T(512)S(1)} all-reduce(f32[512]{0:T(512)S(1)} %fusion), channel_id=1, replica_groups=mesh['grp'=64,'tp'=8] {'tp'}, use_global_device_ids=true, to_apply=%region_5.6 | all-reduce | flops 512 | bytes 4096 | tf_op jit(solution)/shard_map/psum | solution.py:28
  95.6 2.3 fusion.2
  98.1 0.1 reduce.7
  98.3 0.1 select_reduce_fusion.2
  98.7 0.1 select_reduce_fusion
  99.0 2.9 %copy.41 = bf16[8,768,256]{2,1,0:T(8,128)(2,1)} copy(bf16[8,768,256]{1,2,0:T(8,128)(2,1)S(1)} %bitcast.135) | data formatting | bytes 6291456 | tf_op jit(solution)/shard_map/all_to_all | solution.py:32
  101.9 71.0 %all-gather.2.cloned.1.call-done = bf16[512,6144]{1,0:T(8,128)(2,1)} async-done(((bf16[512,768]{1,0:T(8,128)(2,1)}), bf16[512,6144]{1,0:T(8,128)(2,1)}) %all-gather.2.cloned.1.call-update) | async-done | bytes 6291472 | tf_op jit(solution)/shard_map/all_gather | solution.py:35
  172.8 5.5 %convolution_add_fusion = f32[512,256]{0,1:T(8,128)S(1)} fusion(bf16[512,6144]{1,0:T(8,128)(2,1)} %all-gather.2.cloned.1.call-done, bf16[6144,256]{1,0:T(8,128)(2,1)} %bitcast.137, f32[256]{0:T(256)S(1)} %copy-done.6), kind=kOutput, calls=%fused_computation.16 | convolution fusion | flops 1610743808 | bytes 9962496 | tf_op jit(solution)/shard_map/dot_general | solution.py:33
  178.4 0.6 fusion.20
  179.1 0.1 copy.59
  179.2 3.9 %gather_fusion = bf16[1024,256]{1,0:T(8,128)(2,1)S(1)} fusion(bf16[256,512]{0,1:T(8,128)(2,1)S(1)} %copy.59, s32[1024]{0:T(1024)S(1)} %broadcast_clamp_fusion), kind=kCustom, calls=%fused_computation | custom fusion | bytes 1052672 | tf_op jit(solution)/shard_map/jit(_take)/gather | solution.py:82
  183.2 1.1 select_select_fusion
  184.3 19.7 %all-to-all-start.1 = ((bf16[256,64,16]{0,2,1:T(8,128)(2,1)}), bf16[256,64,16]{0,2,1:T(8,128)(2,1)S(1)}, u32[]{:S(2)}, u32[]{:S(2)}) async-start(bf16[256,64,16]{0,2,1:T(8,128)(2,1)} %select_select_fusion), calls=%async_computation.1 | async-start | bytes 1048576 | tf_op jit(solution)/shard_map/all_to_all | solution.py:84
  204.0 0.2 reshape.402
  204.2 0.1 reshape_squeeze.7
  204.4 0.1 select_reduce_fusion.3
  204.5 0.7 fusion.28
  205.3 0.4 fusion.32
  205.9 0.4 fusion.31
  206.3 34.4 %all-to-all-done.1 = bf16[256,64,16]{0,2,1:T(8,128)(2,1)S(1)} async-done(((bf16[256,64,16]{0,2,1:T(8,128)(2,1)}), bf16[256,64,16]{0,2,1:T(8,128)(2,1)S(1)}, u32[]{:S(2)}, u32[]{:S(2)}) %all-to-all-start.1) | async-done | bytes 524320 | tf_op jit(solution)/shard_map/all_to_all | solution.py:84
  240.7 0.1 reshape.406
  240.8 0.7 fusion.29
  241.5 0.4 fusion.33
  242.0 0.7 fusion.26
  242.6 0.2 divide_convert_fusion
  242.9 0.3 fusion.14
  243.1 0.2 fusion.5
  243.4 0.3 fusion.12
  243.7 0.8 convert_element_type.59
  (40 shorter events, 1.1 us)
Async XLA Ops:
  11.3 84.3 %copy-start.5 = (f32[768]{0:T(1024)S(1)}, f32[768]{0:T(1024)}, u32[]{:S(2)}) copy-start(f32[768]{0:T(1024)} %param.10) | copy-start | bytes 9220
  11.3 87.7 %all-to-all-start = ((bf16[768,8,256]{0,2,1:T(8,128)(2,1)}), bf16[768,8,256]{0,2,1:T(8,128)(2,1)S(1)}, u32[]{:S(2)}, u32[]{:S(2)}) async-start(bf16[768,8,256]{0,2,1:T(8,128)(2,1)} %bitcast.136), calls=%async_computation | async-start | bytes 6291456 | tf_op jit(solution)/shard_map/all_to_all | solution.py:32
  20.4 77.5 %copy-start.3 = (s32[64,64]{1,0:T(8,128)S(1)}, s32[64,64]{1,0:T(8,128)}, u32[]{:S(2)}) copy-start(s32[64,64]{1,0:T(8,128)} %param.13) | copy-start | bytes 49156
  20.4 77.8 %copy-start.4 = (s32[64,64]{1,0:T(8,128)S(1)}, s32[64,64]{1,0:T(8,128)}, u32[]{:S(2)}) copy-start(s32[64,64]{1,0:T(8,128)} %param.14) | copy-start | bytes 49156
  20.4 152.4 %all-gather.2.cloned.1.call-start = ((), (), s32[]{:S(2)}) async-start(), calls=%async_computation.2 | async-start | bytes 7077888 | tf_op jit(solution)/shard_map/all_gather | solution.py:35
  99.0 73.9 %copy-start.6 = (f32[256]{0:T(256)S(1)}, f32[256]{0:T(256)}, u32[]{:S(2)}) copy-start(f32[256]{0:T(256)} %param.12) | copy-start | bytes 3076
  179.2 24.8 %copy-start.1 = (bf16[1,64,2,1024]{3,2,1,0:T(2,128)(2,1)S(1)}, bf16[1,64,2,1024]{3,2,1,0:T(2,128)(2,1)}, u32[]{:S(2)}) copy-start(bf16[1,64,2,1024]{3,2,1,0:T(2,128)(2,1)} %param.15) | copy-start | bytes 786436
  179.2 25.0 %copy-start = (bf16[1,64,16,256]{3,2,1,0:T(8,128)(2,1)S(1)}, bf16[1,64,16,256]{3,2,1,0:T(8,128)(2,1)}, u32[]{:S(2)}) copy-start(bf16[1,64,16,256]{3,2,1,0:T(8,128)(2,1)} %param.16) | copy-start | bytes 1572868
  179.2 25.1 %copy-start.2 = (bf16[1,64,2,256]{3,2,1,0:T(2,128)(2,1)S(1)}, bf16[1,64,2,256]{3,2,1,0:T(2,128)(2,1)}, u32[]{:S(2)}) copy-start(bf16[1,64,2,256]{3,2,1,0:T(2,128)(2,1)} %param.17) | copy-start | bytes 196612
  184.3 56.3 %all-to-all-start.1 = ((bf16[256,64,16]{0,2,1:T(8,128)(2,1)}), bf16[256,64,16]{0,2,1:T(8,128)(2,1)S(1)}, u32[]{:S(2)}, u32[]{:S(2)}) async-start(bf16[256,64,16]{0,2,1:T(8,128)(2,1)} %select_select_fusion), calls=%async_computation.1 | async-start | bytes 1048576 | tf_op jit(solution)/shard_map/all_to_all | solution.py:84
Sparse Core Ops, SparseCore 0:
  98.0 74.7 all-gather.1
where the time goes:
time: 252 us; the launch traced here: 251 us
  waiting for transfers between devices  105 us (42%)
  blocking collectives  73.8 us (29%)
  starting transfers between devices  28.9 us (11%)
  local copies, waits for them, and re-layouts  14.7 us (6%)
  between operations  13.7 us (5%)
  matrix products  7.5 us (3%)
  other arithmetic  7.25 us (3%)
    psum x1, blocking collectives, shards(): totals = lax.psum(squares, 'tp')  73.8 us
    all_gather x1, waiting for transfers between devices, shards(): lax.all_gather(normed, 'tp', axis=1, tiled=True)  71 us
    all_to_all x1, waiting for transfers between devices, shards(): lax.all_to_all(outgoing, 'grp', split_axis=1, concat_axis=1, tiled=True)  34.4 us
    all_to_all x1, starting transfers between devices, shards(): lax.all_to_all(outgoing, 'grp', split_axis=1, concat_axis=1, tiled=True)  19.7 us
    all_to_all x1, starting transfers between devices, shards(): lax.all_to_all(kv_weight, 'tp', split_axis=1, concat_axis=0, tiled=True)  9.17 us
    dot_general x1, matrix products, shards(): lax.dot_general(head_weight, lax.all_gather(normed, 'tp', axis=1, tiled=T...  5.54 us
  transfers between devices with their start and end apart: 3, of which 2 were waited for; matrix products, arithmetic and copies ran while one was open for 4% of the time, Pallas kernels for 0%

commit v1 on v0

v1 whole, which is shorter than its diff:
```python
import functools
import math

import jax
import jax.numpy as jnp
import numpy as np
from jax import lax
from jax.experimental import pallas as pl
from jax.experimental.pallas import tpu as pltpu
from jax.sharding import PartitionSpec as P

D = 6144
HD = 128
SLOT = 16
CACHED = 16
STEPS = 2
KVW = 2048
QPK = 8
EPSILON = 1e-06
THETA = 1000000.0

ROWS = 512
FEATS = 768
GRP = 64
TP = 8
CHIPS = 4
WIDTH = 256
HALF = ROWS // 2
SLOTS = GRP * SLOT
MESH = pl.DeviceIdType.MESH
F32 = jnp.float32
BF16 = jnp.bfloat16
NT = (((1,), (1,)), ((), ()))
NN = (((1,), (0,)), ((), ()))


def dot(a, b, dims=NN):
    return lax.dot_general(a, b, dims, preferred_element_type=F32)


def iota(shape, axis):
    return lax.broadcasted_iota(jnp.int32, shape, axis)


def rotary_tables():
    half = HD // 2
    frequency = np.power(np.float32(THETA), -2.0 * np.arange(half, dtype=np.float32) / np.float32(HD)).astype(np.float32)
    angles = ((CACHED + np.arange(SLOT)).astype(np.float32)[:, None] * frequency[None, :]).astype(np.float32)
    cosine, sine = np.cos(angles), np.sin(angles)
    both = np.concatenate([cosine, cosine, -sine, sine], axis=1).astype(np.float32)
    terms, rest = [], both
    for _ in range(3):
        term = rest.astype(jnp.bfloat16)
        terms.append(term)
        rest = rest - term.astype(np.float32)
    table = np.zeros((HD, 3 * 2 * HD), dtype=jnp.bfloat16)
    table[:SLOT] = np.concatenate(terms, axis=1)
    return table


def kernel(
    tokens_hbm, weight_hbm, gain_ref, bias_ref, lengths_ref, dest_ref, query_hbm, old_hbm, new_ref, table_ref,
    out_ref,
    tokens, scaled, weight, query, old,
    pair_out, pair_in, own, from_low, from_high, line_out, final,
    squares, pick, cos_rows, sin_rows, score_old, score_new, outgoing, arrived,
    load_sem, weight_sem, sq_send, sq_recv, pair_send, pair_recv, line_send, low_recv, high_recv, hand_send, hand_recv,
):
    group = lax.axis_index("grp")
    tp = lax.axis_index("tp")
    chip = tp // 2
    core = tp % 2
    partner = tp + 1 - 2 * core

    load_tokens = pltpu.make_async_copy(tokens_hbm, tokens, load_sem.at[0])
    load_tokens.start()

    def head_of(step, whose):
        place = jnp.where(chip < 2, CHIPS - 1 - step, step)
        return place, 2 * place + whose

    def load_weight(step, which):
        whose = (1 - core) if which == 0 else core
        _, head = head_of(step, whose)
        columns = pl.ds(pl.multiple_of(head * WIDTH, WIDTH), WIDTH)
        return pltpu.make_async_copy(weight_hbm.at[:, columns], weight.at[4 * which + step], weight_sem.at[4 * which + step])

    for which in range(2):
        for step in range(CHIPS):
            load_weight(step, which).start()
    load_query = pltpu.make_async_copy(query_hbm, query, load_sem.at[1])
    load_old = pltpu.make_async_copy(old_hbm, old, load_sem.at[2])
    load_query.start()
    load_old.start()

    barrier = pltpu.get_barrier_semaphore()

    def greet_tp(i, carry):
        pl.semaphore_signal(barrier, inc=1, device_id={"tp": (tp + i) % TP}, device_id_type=MESH)
        return carry

    def greet_grp(i, carry):
        pl.semaphore_signal(barrier, inc=1, device_id={"grp": (group + i) % GRP}, device_id_type=MESH)
        return carry

    lax.fori_loop(1, TP, greet_tp, 0)
    lax.fori_loop(1, GRP, greet_grp, 0)

    load_tokens.wait()
    for h in range(2):
        rows = pl.ds(h * HALF, HALF)
        floats = tokens[rows, :].astype(F32)
        scaled[rows, :] = (floats * gain_ref[...]).astype(BF16)
        square = floats * floats
        high = square.astype(BF16)
        low = (square - high.astype(F32)).astype(BF16)
        ones = jnp.ones((8, FEATS), BF16)
        sums = dot(ones, high, NT) + dot(ones, low, NT)
        squares[pl.ds(tp, 1), :, h * HALF:(h + 1) * HALF] = sums[0:1, :].reshape(1, 1, HALF)

    def pair_copy(place):
        return pltpu.make_async_remote_copy(
            src_ref=pair_out.at[place], dst_ref=pair_in.at[place],
            send_sem=pair_send.at[place], recv_sem=pair_recv.at[place],
            device_id={"tp": partner}, device_id_type=MESH,
        )

    def square_copy(i):
        return pltpu.make_async_remote_copy(
            src_ref=squares.at[tp], dst_ref=squares.at[tp],
            send_sem=sq_send.at[i], recv_sem=sq_recv.at[tp],
            device_id={"tp": (tp + i) % TP}, device_id_type=MESH,
        )

    def square_arrival(i):
        source = (tp + i) % TP
        return pltpu.make_async_remote_copy(
            src_ref=squares.at[source], dst_ref=squares.at[source],
            send_sem=sq_send.at[i], recv_sem=sq_recv.at[source],
            device_id={"tp": source}, device_id_type=MESH,
        )

    for step in range(CHIPS):
        place, _ = head_of(step, 0)
        load_weight(step, 0).wait()
        pair_out[pl.ds(place, 1)] = dot(scaled[...], weight[step]).astype(BF16)[None]
        if step == 0:
            pl.semaphore_wait(barrier, TP - 1 + GRP - 1)
        pair_copy(place).start()
    for i in range(1, TP):
        square_copy(i).start()
    for step in range(CHIPS):
        place, _ = head_of(step, 0)
        load_weight(step, 1).wait()
        own[pl.ds(place, 1)] = dot(scaled[...], weight[4 + step])[None]

    def line_copy(direction, place, h):
        rows = pl.ds(h * HALF, HALF)
        landing, sems = (from_low, low_recv) if direction > 0 else (from_high, high_recv)
        return pltpu.make_async_remote_copy(
            src_ref=line_out.at[place, rows], dst_ref=landing.at[place, rows],
            send_sem=line_send.at[place, h], recv_sem=sems.at[place, h],
            device_id={"tp": tp + 2 * direction}, device_id_type=MESH,
        )

    def line_arrival(direction, place, h):
        rows = pl.ds(h * HALF, HALF)
        landing, sems = (from_low, low_recv) if direction > 0 else (from_high, high_recv)
        return pltpu.make_async_remote_copy(
            src_ref=line_out.at[place, rows], dst_ref=landing.at[place, rows],
            send_sem=line_send.at[place, h], recv_sem=sems.at[place, h],
            device_id={"tp": tp - 2 * direction}, device_id_type=MESH,
        )

    def block(place, h):
        rows = pl.ds(h * HALF, HALF)
        return own[place, rows] + pair_in[place, rows].astype(F32)

    def forward(here, direction, place, h):
        rows = pl.ds(h * HALF, HALF)
        first = (here == 0) if direction > 0 else (here == CHIPS - 1)
        value = block(place, h)
        if not first:
            line_arrival(direction, place, h).wait_recv()
            landing = from_low if direction > 0 else from_high
            value = value + landing[place, rows].astype(F32)
        line_out[place, rows] = value.astype(BF16)
        line_copy(direction, place, h).start()

    for here, direction, places in ((0, 1, (3, 2, 1)), (CHIPS - 1, -1, (0, 1, 2))):
        @pl.when(chip == here)
        def _(here=here, direction=direction, places=places):
            for place in places:
                pair_copy(place).wait_recv()
                for h in range(2):
                    forward(here, direction, place, h)

    lengths = lengths_ref[...]
    dests = dest_ref[...]
    mine = iota((GRP, GRP), 0) == group
    own_lengths = jnp.sum(jnp.where(mine, lengths, 0), axis=0, keepdims=True)
    own_dest = jnp.sum(jnp.where(mine, dests, 0), axis=0, keepdims=True)
    before = (iota((GRP, GRP), 0) < iota((GRP, GRP), 1)).astype(F32)
    spread = jnp.broadcast_to(own_lengths.astype(F32), (8, GRP))
    starts = dot(spread, before)[0:1, :].astype(jnp.int32)
    routed = own_dest == iota((GRP, GRP), 0)
    slot_first = jnp.sum(jnp.where(routed, starts, 0), axis=1, keepdims=True)
    slot_length = jnp.sum(jnp.where(routed, own_lengths, 0), axis=1, keepdims=True)
    for part in range(8):
        requests = slice(part * 8, part * 8 + 8)
        offset = iota((8, SLOT, ROWS), 1)
        first = slot_first[requests][:, :, None]
        length = slot_length[requests][:, :, None]
        hit = (iota((8, SLOT, ROWS), 2) == first + offset) & (offset < length)
        pick[part * 128:part * 128 + 128, :] = hit.astype(F32).reshape(128, ROWS).astype(BF16)

    row_index = iota((ROWS, GRP), 0)
    first_row = jnp.max(jnp.where(starts <= row_index, starts, 0), axis=1, keepdims=True)
    at_offset = (iota((ROWS, HD), 1) + first_row == iota((ROWS, HD), 0)).astype(F32).astype(BF16)
    tabled = dot(at_offset, table_ref[...])
    cos_rows[...] = tabled[:, 0:128] + tabled[:, 256:384] + tabled[:, 512:640]
    sin_rows[...] = tabled[:, 128:256] + tabled[:, 384:512] + tabled[:, 640:768]

    toward_me = dests == group
    live = jnp.sum(jnp.where(toward_me, lengths, 0), axis=1, keepdims=True)
    at_source = iota((GRP, SLOTS), 1) // SLOT == iota((GRP, SLOTS), 0)
    live_lanes = jnp.sum(jnp.where(at_source, live, 0), axis=0, keepdims=True)
    live_lanes = (iota((1, SLOTS), 1) % SLOT < live_lanes).astype(F32)

    load_query.wait()
    load_old.wait()
    scale = 1.0 / math.sqrt(HD)
    same = iota((128, 128), 0) // 16 == iota((128, 128), 1) // 16
    same_new = (iota((128, 16), 0) // 16 == iota((128, 16), 1) // 2) & (iota((128, 16), 1) % 2 <= iota((128, 16), 0) % 2)
    for part in range(8):
        rows = slice(part * 128, part * 128 + 128)
        new_rows = slice(part * 16, part * 16 + 16)
        score_old[rows, :] = jnp.where(same, dot(query[rows, :], old[rows, 0:HD], NT) * scale, -1e30)
        score_new[rows, :] = jnp.where(same_new, dot(query[rows, :], new_ref[new_rows, 0:HD], NT) * scale, -1e30)

    schedules = {
        0: [(-1, 0, 0), (-1, 0, 1)],
        1: [(1, 3, 0), (1, 3, 1), (-1, 0, 0), (1, 2, 0), (-1, 0, 1), (1, 2, 1), (-1, 1, 0), (-1, 1, 1), (1, 1, 0), (1, 1, 1)],
        2: [(-1, 0, 0), (-1, 0, 1), (1, 3, 0), (-1, 1, 0), (1, 3, 1), (-1, 1, 1), (1, 2, 0), (1, 2, 1), (-1, 2, 0), (-1, 2, 1)],
        3: [(1, 3, 0), (1, 3, 1)],
    }
    for here in range(CHIPS):
        @pl.when(chip == here)
        def _(here=here):
            have = {0: {3, 2, 1}, 3: {0, 1, 2}}.get(here, set())
            begun = set()
            for direction, place, h in schedules[here]:
                if place not in have:
                    have.add(place)
                    pair_copy(place).wait_recv()
                rows = pl.ds(h * HALF, HALF)
                if place != here:
                    forward(here, direction, place, h)
                    continue
                value = final[rows, :] if h in begun else block(place, h)
                begun.add(h)
                line_arrival(direction, place, h).wait_recv()
                landing = from_low if direction > 0 else from_high
                final[rows, :] = value + landing[place, rows].astype(F32)

    for i in range(1, TP):
        square_arrival(i).wait_recv()
    total = jnp.sum(squares[...].reshape(TP, ROWS), axis=0, keepdims=True)
    inv_rms = lax.rsqrt(total / D + EPSILON)
    inv_rms = jnp.broadcast_to(inv_rms, (HD, ROWS)).T
    keys = final[:, 0:HD] * inv_rms + bias_ref[:, 0:HD]
    values = final[:, HD:WIDTH] * inv_rms + bias_ref[:, HD:WIDTH]
    turned = pltpu.roll(keys, HD // 2, 1)
    keys = (keys * cos_rows[...] + turned * sin_rows[...]).astype(BF16)
    handed = jnp.concatenate([keys, values.astype(BF16)], axis=1)
    outgoing[...] = dot(pick[...], handed).astype(BF16)

    y, x, z = group // 16, (group // 4) % 4, group % 4

    def hand_copy(away, i):
        target = ((y + i // 4) % 4 * 4 + (x + i % 4) % 4) * 4 + (z + away) % 4
        return pltpu.make_async_remote_copy(
            src_ref=outgoing.at[pl.ds(target * SLOT, SLOT)], dst_ref=arrived.at[pl.ds(group * SLOT, SLOT)],
            send_sem=hand_send.at[away * 16 + i], recv_sem=hand_recv.at[away * 16 + i],
            device_id={"grp": target}, device_id_type=MESH,
        )

    def hand_arrival(away, i):
        source = ((y + 4 - i // 4) % 4 * 4 + (x + 4 - i % 4) % 4) * 4 + (z + 4 - away) % 4
        return pltpu.make_async_remote_copy(
            src_ref=outgoing.at[pl.ds(source * SLOT, SLOT)], dst_ref=arrived.at[pl.ds(source * SLOT, SLOT)],
            send_sem=hand_send.at[away * 16 + i], recv_sem=hand_recv.at[away * 16 + i],
            device_id={"grp": source}, device_id_type=MESH,
        )

    def send(away):
        def body(i, carry):
            hand_copy(away, i).start()
            return carry
        return body

    def receive(away):
        def body(i, carry):
            hand_arrival(away, i).wait_recv()
            return carry
        return body

    def sent(away):
        def body(i, carry):
            hand_copy(away, i).wait_send()
            return carry
        return body

    for away in (2, 1, 3, 0):
        lax.fori_loop(0 if away else 1, 16, send(away), 0)
    own_rows = pl.ds(pl.multiple_of(group * SLOT, SLOT), SLOT)
    arrived[own_rows, :] = outgoing[own_rows, :]
    for away in (0, 1, 3, 2):
        lax.fori_loop(0 if away else 1, 16, receive(away), 0)

    for part in range(8):
        rows = slice(part * 128, part * 128 + 128)
        new_rows = slice(part * 16, part * 16 + 16)
        span_live = same & (live_lanes[:, rows] > 0.5)
        cached, fresh = score_old[rows, :], score_new[rows, :]
        span = jnp.where(span_live, dot(query[rows, :], arrived[rows, 0:HD], NT) * scale, -1e30)
        top = jnp.maximum(jnp.max(jnp.maximum(cached, span), axis=1, keepdims=True), jnp.max(fresh, axis=1, keepdims=True))
        cached, span, fresh = jnp.exp(cached - top), jnp.exp(span - top), jnp.exp(fresh - top)
        weight_sum = jnp.sum(cached + span, axis=1, keepdims=True) + jnp.sum(fresh, axis=1, keepdims=True)
        inverse = 1.0 / weight_sum
        result = dot((cached * inverse).astype(BF16), old[rows, HD:WIDTH])
        result = result + dot((span * inverse).astype(BF16), arrived[rows, HD:WIDTH])
        result = result + dot((fresh * inverse).astype(BF16), new_ref[new_rows, HD:WIDTH])
        out_ref[rows, :] = result.astype(BF16)

    for place in range(CHIPS):
        pair_copy(place).wait_send()
        for h in range(2):
            @pl.when(chip != place)
            def _(place=place, h=h):
                rows = pl.ds(h * HALF, HALF)
                pltpu.make_async_remote_copy(
                    src_ref=line_out.at[place, rows], dst_ref=from_low.at[place, rows],
                    send_sem=line_send.at[place, h], recv_sem=low_recv.at[place, h],
                    device_id={"tp": partner}, device_id_type=MESH,
                ).wait_send()
    for i in range(1, TP):
        square_copy(i).wait_send()
    for away in (0, 1, 3, 2):
        lax.fori_loop(0 if away else 1, 16, sent(away), 0)


def shards(tokens, gain, kv_weight, kv_bias, lengths, dest, queries, old_cache, new_kv):
    query_rows = queries.reshape(GRP, STEPS, QPK, HD).transpose(0, 2, 1, 3).reshape(SLOTS, HD)
    any_space = pl.BlockSpec(memory_space=pl.ANY)
    vmem = pl.BlockSpec(memory_space=pltpu.VMEM)
    dma = pltpu.SemaphoreType.DMA
    out = pl.pallas_call(
        kernel,
        out_shape=jax.ShapeDtypeStruct((SLOTS, HD), BF16),
        in_specs=[any_space, any_space, vmem, vmem, vmem, vmem, any_space, any_space, vmem, vmem],
        out_specs=vmem,
        scratch_shapes=[
            pltpu.VMEM((ROWS, FEATS), BF16),
            pltpu.VMEM((ROWS, FEATS), BF16),
            pltpu.VMEM((TP, FEATS, WIDTH), BF16),
            pltpu.VMEM((SLOTS, HD), BF16),
            pltpu.VMEM((SLOTS, WIDTH), BF16),
            pltpu.VMEM((CHIPS, ROWS, WIDTH), BF16),
            pltpu.VMEM((CHIPS, ROWS, WIDTH), BF16),
            pltpu.VMEM((CHIPS, ROWS, WIDTH), F32),
            pltpu.VMEM((CHIPS, ROWS, WIDTH), BF16),
            pltpu.VMEM((CHIPS, ROWS, WIDTH), BF16),
            pltpu.VMEM((CHIPS, ROWS, WIDTH), BF16),
            pltpu.VMEM((ROWS, WIDTH), F32),
            pltpu.VMEM((TP, 1, ROWS), F32),
            pltpu.VMEM((SLOTS, ROWS), BF16),
            pltpu.VMEM((ROWS, HD), F32),
            pltpu.VMEM((ROWS, HD), F32),
            pltpu.VMEM((SLOTS, 128), F32),
            pltpu.VMEM((SLOTS, 16), F32),
            pltpu.VMEM((SLOTS, WIDTH), BF16),
            pltpu.VMEM((SLOTS, WIDTH), BF16),
            dma((3,)),
            dma((TP,)),
            dma((TP,)),
            dma((TP,)),
            dma((CHIPS,)),
            dma((CHIPS,)),
            dma((CHIPS, 2)),
            dma((CHIPS, 2)),
            dma((CHIPS, 2)),
            dma((GRP,)),
            dma((GRP,)),
        ],
        compiler_params=pltpu.CompilerParams(
            collective_id=0, has_side_effects=True, vmem_limit_bytes=48 * 1024 * 1024
        ),
        cost_estimate=pl.CostEstimate(flops=2_500_000_000, bytes_accessed=6_000_000, transcendentals=300_000),
    )(
        tokens, kv_weight, gain.reshape(1, FEATS), kv_bias.reshape(1, WIDTH), lengths, dest,
        query_rows, old_cache.reshape(SLOTS, WIDTH), new_kv.reshape(GRP * STEPS, WIDTH), jnp.asarray(rotary_tables()),
    )
    return out.reshape(GRP, QPK, STEPS, HD).transpose(0, 2, 1, 3).reshape(1, GRP, STEPS, QPK * HD)


def solution(mesh):
    return jax.shard_map(
        shards,
        mesh=mesh,
        in_specs=(
            P("grp", "tp"),
            P("tp"),
            P("tp", None),
            P("tp"),
            P(),
            P(),
            P("grp", None, None, "tp"),
            P("grp", None, None, "tp"),
            P("grp", None, None, "tp"),
        ),
        out_specs=P("grp", None, None, "tp"),
        check_vma=False,
    )
```

time: 252 us -> 82.8 us (0.33)
  waiting for transfers between devices: 105 us -> 0 us
  blocking collectives: 73.8 us -> 0 us
  Pallas kernels: 0 us -> 71.9 us
  starting transfers between devices: 28.9 us -> 0 us
  between operations: 13.7 us -> 0.03 us
  matrix products: 7.5 us -> 0 us
  other arithmetic: 7.25 us -> 0 us
  local copies, waits for them, and re-layouts: 14.7 us -> 10.4 us
    psum x1 -> x0, blocking collectives: 73.8 us -> none  [shards(): totals = lax.psum(squares, 'tp')]
    pallas_call x0 -> x1, Pallas kernels: none -> 71.9 us  [shards(): pl.pallas_call(kernel, out_shape=jax.ShapeDtypeStruct((SLOTS, HD), BF16),...]
    all_gather x1 -> x0, waiting for transfers between devices: 71 us -> none  [shards(): lax.all_gather(normed, 'tp', axis=1, tiled=True)]
    all_to_all x2 -> x0, waiting for transfers between devices: 34.4 us -> none  [the longest x1 34.4 us: shards(): lax.all_to_all(outgoing, 'grp', split_axis=1, concat_axis=1, tiled=True)]
    all_to_all x2 -> x0, starting transfers between devices: 28.9 us -> none  [the longest x1 19.7 us: shards(): lax.all_to_all(outgoing, 'grp', split_axis=1, concat_axis=1, tiled=True)]
    dot_general x7 -> x0, matrix products: 7.5 us -> none  [the longest x1 5.54 us: shards(): lax.dot_general(head_weight, lax.all_gather(normed, 'tp', axis=1, tiled=T...]
    unnamed x15 -> x17, local copies, waits for them, and re-layouts: 4.77 us -> 8.83 us
    gather x1 -> x0, local copies, waits for them, and re-layouts: 3.94 us -> none  [shards(): jnp.take(key_values, picked_rows, axis=1)]
  transfers between devices with their start and end apart: 3 -> 0, of which waited for: 2 -> 0; matrix products, arithmetic and copies ran while one was open for 4% -> 0% of each run, Pallas kernels for 0% -> 0%
where the time goes in v1:
time: 82.8 us; the launch traced here: 82.3 us
  Pallas kernels  71.9 us (87%)
  local copies, waits for them, and re-layouts  10.4 us (13%)
    pallas_call x1, Pallas kernels, shards(): pl.pallas_call(kernel, out_shape=jax.ShapeDtypeStruct((SLOTS, HD), BF16),...  71.9 us
    unnamed x17, local copies, waits for them, and re-layouts  8.83 us

profile of v1, /device:TPU:32, one launch (start us, length us, event | category | flops | bytes accessed | tf_op | source)
XLA Modules:
  0.0 82.3 jit_solution(9814821224136717500)
XLA Ops:
  0.0 0.7 reshape.24.gain_ref
  0.7 0.9 %reshape.29.new_ref = bf16[128,256]{1,0:T(8,128)(2,1)S(1)} reshape(bf16[1,64,2,256]{3,2,1,0:T(2,128)(2,1)} %param.18) | data formatting | bytes 131072 | tf_op jit(solution)/shard_map/reshape | solution.py:402
  1.6 0.0 copy-start
  1.6 1.9 %copy-done = bf16[768,2048]{1,0:T(8,128)(2,1)S(1)} copy-done((bf16[768,2048]{1,0:T(8,128)(2,1)S(1)}, bf16[768,2048]{1,0:T(8,128)(2,1)}, u32[]{:S(2)}) %copy-start) | copy-done | bytes 3145752
  3.5 0.0 copy-start.1
  3.5 1.1 %copy-done.1 = bf16[512,768]{1,0:T(8,128)(2,1)S(1)} copy-done((bf16[512,768]{1,0:T(8,128)(2,1)S(1)}, bf16[512,768]{1,0:T(8,128)(2,1)}, u32[]{:S(2)}) %copy-start.1) | copy-done | bytes 786456
  4.6 0.0 copy-start.2
  4.6 1.0 %copy-done.2 = bf16[1,64,16,256]{3,2,1,0:T(8,128)(2,1)S(1)} copy-done((bf16[1,64,16,256]{3,2,1,0:T(8,128)(2,1)S(1)}, bf16[1,64,16,256]{3,2,1,0:T(8,128)(2,1)}, u32[]{:S(2)}) %copy-start.2) | copy-done | bytes 524312
  5.6 0.0 copy-start.3
  5.6 0.9 %copy-done.3 = bf16[1,64,2,1024]{3,2,1,0:T(2,128)(2,1)S(1)} copy-done((bf16[1,64,2,1024]{3,2,1,0:T(2,128)(2,1)S(1)}, bf16[1,64,2,1024]{3,2,1,0:T(2,128)(2,1)}, u32[]{:S(2)}) %copy-start.3) | copy-done | bytes 262168
  6.6 0.0 copy-start.4
  6.6 0.8 copy-done.4
  7.3 0.0 copy-start.5
  7.3 0.8 copy-done.5
  8.1 0.0 copy-start.6
  8.1 0.7 copy-done.6
  8.8 0.0 copy-start.7
  8.8 0.9 %copy-done.7 = bf16[128,768]{1,0:T(8,128)(2,1)S(1)} copy-done((bf16[128,768]{1,0:T(8,128)(2,1)S(1)}, bf16[128,768]{1,0:T(8,128)(2,1)}, u32[]{:S(2)}) %copy-start.7) | copy-done | bytes 196632
  9.7 71.9 %shard_map.100 = bf16[1024,128]{1,0:T(8,128)(2,1)S(1)} custom-call(bf16[512,768]{1,0:T(8,128)(2,1)S(1)} %copy-done.1, bf16[768,2048]{1,0:T(8,128)(2,1)S(1)} %copy-done, f32[1,768]{1,0:T(1,128)S(1)} %reshape.24.gain_ref, f32[1,256]{1,0:T(1,128)S(1)} %bitcast.15, s32[64,64]{1,0:T(8,128)S(1)} %copy-done.4, s32[64,64]{1,0:T(8,128)S(1)} %copy-done.5, ...), custom_call_target="tpu_custom_call" | custom-call | flops 2500000000 | bytes 6000000 | tf_op jit(solution)/shard_map/pallas_call | solution.py:358
  81.6 0.7 copy.14
Async XLA Ops:
  1.6 1.9 %copy-start = (bf16[768,2048]{1,0:T(8,128)(2,1)S(1)}, bf16[768,2048]{1,0:T(8,128)(2,1)}, u32[]{:S(2)}) copy-start(bf16[768,2048]{1,0:T(8,128)(2,1)} %weight_hbm.1) | copy-start | bytes 9437188
  3.5 1.1 %copy-start.1 = (bf16[512,768]{1,0:T(8,128)(2,1)S(1)}, bf16[512,768]{1,0:T(8,128)(2,1)}, u32[]{:S(2)}) copy-start(bf16[512,768]{1,0:T(8,128)(2,1)} %tokens_hbm.1) | copy-start | bytes 2359300
  4.6 1.0 %copy-start.2 = (bf16[1,64,16,256]{3,2,1,0:T(8,128)(2,1)S(1)}, bf16[1,64,16,256]{3,2,1,0:T(8,128)(2,1)}, u32[]{:S(2)}) copy-start(bf16[1,64,16,256]{3,2,1,0:T(8,128)(2,1)} %param.17) | copy-start | bytes 1572868
  5.6 0.9 %copy-start.3 = (bf16[1,64,2,1024]{3,2,1,0:T(2,128)(2,1)S(1)}, bf16[1,64,2,1024]{3,2,1,0:T(2,128)(2,1)}, u32[]{:S(2)}) copy-start(bf16[1,64,2,1024]{3,2,1,0:T(2,128)(2,1)} %param.16) | copy-start | bytes 786436
  6.6 0.8 copy-start.4
  7.3 0.8 copy-start.5
  8.1 0.7 copy-start.6
  8.8 0.9 %copy-start.7 = (bf16[128,768]{1,0:T(8,128)(2,1)S(1)}, bf16[128,768]{1,0:T(8,128)(2,1)}, u32[]{:S(2)}) copy-start(bf16[128,768]{1,0:T(8,128)(2,1)} %constant.2.clone.table_ref) | copy-start | bytes 589828

commit v2 on v1

--- a/solution.py
+++ b/solution.py
@@ -47,21 +47,13 @@
     frequency = np.power(np.float32(THETA), -2.0 * np.arange(half, dtype=np.float32) / np.float32(HD)).astype(np.float32)
     angles = ((CACHED + np.arange(SLOT)).astype(np.float32)[:, None] * frequency[None, :]).astype(np.float32)
     cosine, sine = np.cos(angles), np.sin(angles)
-    both = np.concatenate([cosine, cosine, -sine, sine], axis=1).astype(np.float32)
-    terms, rest = [], both
-    for _ in range(3):
-        term = rest.astype(jnp.bfloat16)
-        terms.append(term)
-        rest = rest - term.astype(np.float32)
-    table = np.zeros((HD, 3 * 2 * HD), dtype=jnp.bfloat16)
-    table[:SLOT] = np.concatenate(terms, axis=1)
-    return table
+    return np.concatenate([cosine, cosine, -sine, sine], axis=1).astype(np.float32)
 
 
 def kernel(
-    tokens_hbm, weight_hbm, gain_ref, bias_ref, lengths_ref, dest_ref, query_hbm, old_hbm, new_ref, table_ref,
+    tokens_hbm, weight_hbm, gain_hbm, bias_hbm, lengths_hbm, dest_hbm, query_hbm, old_hbm, new_hbm, table_hbm,
     out_ref,
-    tokens, scaled, weight, query, old,
+    tokens, scaled, weight, gain_ref, bias_ref, lengths_ref, dest_ref, query, old, new_ref, new_values, table_ref,
     pair_out, pair_in, own, from_low, from_high, line_out, final,
     squares, pick, cos_rows, sin_rows, score_old, score_new, outgoing, arrived,
     load_sem, weight_sem, sq_send, sq_recv, pair_send, pair_recv, line_send, low_recv, high_recv, hand_send, hand_recv,
@@ -72,7 +64,9 @@
     core = tp % 2
     partner = tp + 1 - 2 * core
 
-    load_tokens = pltpu.make_async_copy(tokens_hbm, tokens, load_sem.at[0])
+    load_gain = pltpu.make_async_copy(gain_hbm, gain_ref, load_sem.at[0])
+    load_tokens = pltpu.make_async_copy(tokens_hbm, tokens, load_sem.at[1])
+    load_gain.start()
     load_tokens.start()
 
     def head_of(step, whose):
@@ -88,10 +82,15 @@
     for which in range(2):
         for step in range(CHIPS):
             load_weight(step, which).start()
-    load_query = pltpu.make_async_copy(query_hbm, query, load_sem.at[1])
-    load_old = pltpu.make_async_copy(old_hbm, old, load_sem.at[2])
-    load_query.start()
-    load_old.start()
+    later_loads = [
+        pltpu.make_async_copy(source, target, load_sem.at[2 + i])
+        for i, (source, target) in enumerate((
+            (lengths_hbm, lengths_ref), (dest_hbm, dest_ref), (table_hbm, table_ref), (bias_hbm, bias_ref),
+            (query_hbm, query), (old_hbm, old), (new_hbm, new_ref),
+        ))
+    ]
+    for load in later_loads:
+        load.start()
 
     barrier = pltpu.get_barrier_semaphore()
 
@@ -106,11 +105,12 @@
     lax.fori_loop(1, TP, greet_tp, 0)
     lax.fori_loop(1, GRP, greet_grp, 0)
 
+    load_gain.wait()
     load_tokens.wait()
     for h in range(2):
         rows = pl.ds(h * HALF, HALF)
         floats = tokens[rows, :].astype(F32)
-        scaled[rows, :] = (floats * gain_ref[...]).astype(BF16)
+        scaled[rows, :] = (floats * gain_ref[...][None, :]).astype(BF16)
         square = floats * floats
         high = square.astype(BF16)
         low = (square - high.astype(F32)).astype(BF16)
@@ -195,6 +195,8 @@
                 for h in range(2):
                     forward(here, direction, place, h)
 
+    for load in later_loads:
+        load.wait()
     lengths = lengths_ref[...]
     dests = dest_ref[...]
     mine = iota((GRP, GRP), 0) == group
@@ -216,10 +218,15 @@
 
     row_index = iota((ROWS, GRP), 0)
     first_row = jnp.max(jnp.where(starts <= row_index, starts, 0), axis=1, keepdims=True)
-    at_offset = (iota((ROWS, HD), 1) + first_row == iota((ROWS, HD), 0)).astype(F32).astype(BF16)
-    tabled = dot(at_offset, table_ref[...])
-    cos_rows[...] = tabled[:, 0:128] + tabled[:, 256:384] + tabled[:, 512:640]
-    sin_rows[...] = tabled[:, 128:256] + tabled[:, 384:512] + tabled[:, 640:768]
+    at_offset = (iota((ROWS, SLOT), 1) + first_row == iota((ROWS, SLOT), 0)).astype(F32).astype(BF16)
+    rest = table_ref[...]
+    tabled = jnp.zeros((ROWS, 2 * HD), F32)
+    for _ in range(3):
+        term = rest.astype(BF16)
+        rest = rest - term.astype(F32)
+        tabled = tabled + dot(at_offset, term)
+    cos_rows[...] = tabled[:, 0:HD]
+    sin_rows[...] = tabled[:, HD:2 * HD]
 
     toward_me = dests == group
     live = jnp.sum(jnp.where(toward_me, lengths, 0), axis=1, keepdims=True)
@@ -227,16 +234,15 @@
     live_lanes = jnp.sum(jnp.where(at_source, live, 0), axis=0, keepdims=True)
     live_lanes = (iota((1, SLOTS), 1) % SLOT < live_lanes).astype(F32)
 
-    load_query.wait()
-    load_old.wait()
+    new_values[...] = pltpu.roll(new_ref[...].astype(F32), 4 * GRP - 2, 0).astype(BF16)
     scale = 1.0 / math.sqrt(HD)
     same = iota((128, 128), 0) // 16 == iota((128, 128), 1) // 16
-    same_new = (iota((128, 16), 0) // 16 == iota((128, 16), 1) // 2) & (iota((128, 16), 1) % 2 <= iota((128, 16), 0) % 2)
+    same_new = (iota((128, 32), 0) // 16 == iota((128, 32), 1) // 4) & (iota((128, 32), 1) % 4 <= iota((128, 32), 0) % 2)
     for part in range(8):
         rows = slice(part * 128, part * 128 + 128)
-        new_rows = slice(part * 16, part * 16 + 16)
+        new_rows = slice(part * 32, part * 32 + 32)
         score_old[rows, :] = jnp.where(same, dot(query[rows, :], old[rows, 0:HD], NT) * scale, -1e30)
-        score_new[rows, :] = jnp.where(same_new, dot(query[rows, :], new_ref[new_rows, 0:HD], NT) * scale, -1e30)
+        score_new[rows, :] = jnp.where(same_new, dot(query[rows, :], new_ref[new_rows, :], NT) * scale, -1e30)
 
     schedules = {
         0: [(-1, 0, 0), (-1, 0, 1)],
@@ -268,8 +274,8 @@
     total = jnp.sum(squares[...].reshape(TP, ROWS), axis=0, keepdims=True)
     inv_rms = lax.rsqrt(total / D + EPSILON)
     inv_rms = jnp.broadcast_to(inv_rms, (HD, ROWS)).T
-    keys = final[:, 0:HD] * inv_rms + bias_ref[:, 0:HD]
-    values = final[:, HD:WIDTH] * inv_rms + bias_ref[:, HD:WIDTH]
+    keys = final[:, 0:HD] * inv_rms + bias_ref[0:HD][None, :]
+    values = final[:, HD:WIDTH] * inv_rms + bias_ref[HD:WIDTH][None, :]
     turned = pltpu.roll(keys, HD // 2, 1)
     keys = (keys * cos_rows[...] + turned * sin_rows[...]).astype(BF16)
     handed = jnp.concatenate([keys, values.astype(BF16)], axis=1)
@@ -320,7 +326,7 @@
 
     for part in range(8):
         rows = slice(part * 128, part * 128 + 128)
-        new_rows = slice(part * 16, part * 16 + 16)
+        new_rows = slice(part * 32, part * 32 + 32)
         span_live = same & (live_lanes[:, rows] > 0.5)
         cached, fresh = score_old[rows, :], score_new[rows, :]
         span = jnp.where(span_live, dot(query[rows, :], arrived[rows, 0:HD], NT) * scale, -1e30)
@@ -330,7 +336,7 @@
         inverse = 1.0 / weight_sum
         result = dot((cached * inverse).astype(BF16), old[rows, HD:WIDTH])
         result = result + dot((span * inverse).astype(BF16), arrived[rows, HD:WIDTH])
-        result = result + dot((fresh * inverse).astype(BF16), new_ref[new_rows, HD:WIDTH])
+        result = result + dot((fresh * inverse).astype(BF16), new_values[new_rows, :])
         out_ref[rows, :] = result.astype(BF16)
 
     for place in range(CHIPS):
@@ -352,20 +358,28 @@
 
 def shards(tokens, gain, kv_weight, kv_bias, lengths, dest, queries, old_cache, new_kv):
     query_rows = queries.reshape(GRP, STEPS, QPK, HD).transpose(0, 2, 1, 3).reshape(SLOTS, HD)
+    new_rows = new_kv.reshape(GRP, STEPS, 2, HD).transpose(0, 2, 1, 3).reshape(4 * GRP, HD)
     any_space = pl.BlockSpec(memory_space=pl.ANY)
     vmem = pl.BlockSpec(memory_space=pltpu.VMEM)
     dma = pltpu.SemaphoreType.DMA
     out = pl.pallas_call(
         kernel,
         out_shape=jax.ShapeDtypeStruct((SLOTS, HD), BF16),
-        in_specs=[any_space, any_space, vmem, vmem, vmem, vmem, any_space, any_space, vmem, vmem],
+        in_specs=[any_space] * 10,
         out_specs=vmem,
         scratch_shapes=[
             pltpu.VMEM((ROWS, FEATS), BF16),
             pltpu.VMEM((ROWS, FEATS), BF16),
             pltpu.VMEM((TP, FEATS, WIDTH), BF16),
+            pltpu.VMEM((FEATS,), F32),
+            pltpu.VMEM((WIDTH,), F32),
+            pltpu.VMEM((GRP, GRP), jnp.int32),
+            pltpu.VMEM((GRP, GRP), jnp.int32),
             pltpu.VMEM((SLOTS, HD), BF16),
             pltpu.VMEM((SLOTS, WIDTH), BF16),
+            pltpu.VMEM((4 * GRP, HD), BF16),
+            pltpu.VMEM((4 * GRP, HD), BF16),
+            pltpu.VMEM((SLOT, 2 * HD), F32),
             pltpu.VMEM((CHIPS, ROWS, WIDTH), BF16),
             pltpu.VMEM((CHIPS, ROWS, WIDTH), BF16),
             pltpu.VMEM((CHIPS, ROWS, WIDTH), F32),
@@ -378,10 +392,10 @@
             pltpu.VMEM((ROWS, HD), F32),
             pltpu.VMEM((ROWS, HD), F32),
             pltpu.VMEM((SLOTS, 128), F32),
-            pltpu.VMEM((SLOTS, 16), F32),
+            pltpu.VMEM((SLOTS, 32), F32),
             pltpu.VMEM((SLOTS, WIDTH), BF16),
             pltpu.VMEM((SLOTS, WIDTH), BF16),
-            dma((3,)),
+            dma((9,)),
             dma((TP,)),
             dma((TP,)),
             dma((TP,)),
@@ -394,12 +408,12 @@
             dma((GRP,)),
         ],
         compiler_params=pltpu.CompilerParams(
-            collective_id=0, has_side_effects=True, vmem_limit_bytes=48 * 1024 * 1024
+            collective_id=0, has_side_effects=True, vmem_limit_bytes=60 * 1024 * 1024
         ),
         cost_estimate=pl.CostEstimate(flops=2_500_000_000, bytes_accessed=6_000_000, transcendentals=300_000),
     )(
-        tokens, kv_weight, gain.reshape(1, FEATS), kv_bias.reshape(1, WIDTH), lengths, dest,
-        query_rows, old_cache.reshape(SLOTS, WIDTH), new_kv.reshape(GRP * STEPS, WIDTH), jnp.asarray(rotary_tables()),
+        tokens, kv_weight, gain, kv_bias, lengths, dest,
+        query_rows, old_cache.reshape(SLOTS, WIDTH), new_rows, jnp.asarray(rotary_tables()),
     )
     return out.reshape(GRP, QPK, STEPS, HD).transpose(0, 2, 1, 3).reshape(1, GRP, STEPS, QPK * HD)
 

time: 82.8 us -> 74.2 us (0.90)
  local copies, waits for them, and re-layouts: 10.4 us -> 1.83 us
    unnamed x17 -> x1, local copies, waits for them, and re-layouts: 8.83 us -> 1.83 us
    reshape x2 -> x0, local copies, waits for them, and re-layouts: 1.56 us -> none  [the longest x1 0.87 us: shards(): new_kv.reshape(GRP * STEPS, WIDTH)]
where the time goes in v2:
time: 74.2 us; the launch traced here: 74.1 us
  Pallas kernels  72.2 us (97%)
  local copies, waits for them, and re-layouts  1.83 us (2%)
    pallas_call x1, Pallas kernels, shards(): pl.pallas_call(kernel, out_shape=jax.ShapeDtypeStruct((SLOTS, HD), BF16),...  72.2 us
    unnamed x1, local copies, waits for them, and re-layouts  1.83 us

profile of v2, /device:TPU:32, one launch (start us, length us, event | category | flops | bytes accessed | tf_op | source)
XLA Modules:
  0.0 74.1 jit_solution(1214712630466066239)
XLA Ops:
  0.0 72.2 %shard_map.100 = bf16[1024,128]{1,0:T(8,128)(2,1)} custom-call(bf16[512,768]{1,0:T(8,128)(2,1)} %tokens_hbm.1, bf16[768,2048]{1,0:T(8,128)(2,1)} %weight_hbm.1, f32[768]{0:T(1024)} %gain_hbm.1, f32[256]{0:T(256)} %bias_hbm.1, s32[64,64]{1,0:T(8,128)} %lengths_hbm.1, s32[64,64]{1,0:T(8,128)} %dest_hbm.1, bf16[1024,128]{1,0:T(8,128)(2,1)} %bitcast.18, ...), custom_call_target="tpu_custom_call" | custom-call | flops 2500000000 | bytes 6000000 | tf_op jit(solution)/shard_map/pallas_call | solution.py:365
  72.3 1.8 %copy.15 = bf16[1,64,2,1024]{3,2,1,0:T(2,128)(2,1)} copy(bf16[1,64,2,1024]{3,2,1,0:T(2,128)(2,1)} %bitcast.16) | data formatting | bytes 524288

commit v3 on v2

v3 whole, which is shorter than its diff:
```python
import functools
import math

import jax
import jax.numpy as jnp
import numpy as np
from jax import lax
from jax.experimental import pallas as pl
from jax.experimental.pallas import tpu as pltpu
from jax.sharding import PartitionSpec as P

D = 6144
HD = 128
SLOT = 16
CACHED = 16
STEPS = 2
KVW = 2048
QPK = 8
EPSILON = 1e-06
THETA = 1000000.0

ROWS = 512
FEATS = 768
GRP = 64
TP = 8
CHIPS = 4
WIDTH = 256
HALF = ROWS // 2
SLOTS = GRP * SLOT
LAYERS = 4
PLANE = GRP // LAYERS
LANES = PLANE * SLOT
LEADER = 7
MESH = pl.DeviceIdType.MESH
F32 = jnp.float32
BF16 = jnp.bfloat16
NT = (((1,), (1,)), ((), ()))
NN = (((1,), (0,)), ((), ()))


def dot(a, b, dims=NN):
    return lax.dot_general(a, b, dims, preferred_element_type=F32)


def iota(shape, axis):
    return lax.broadcasted_iota(jnp.int32, shape, axis)


def rotary_tables():
    half = HD // 2
    frequency = np.power(np.float32(THETA), -2.0 * np.arange(half, dtype=np.float32) / np.float32(HD)).astype(np.float32)
    angles = ((CACHED + np.arange(SLOT)).astype(np.float32)[:, None] * frequency[None, :]).astype(np.float32)
    cosine, sine = np.cos(angles), np.sin(angles)
    return np.concatenate([cosine, cosine, -sine, sine], axis=1).astype(np.float32)


def kernel(
    tokens_hbm, weight_hbm, gain_hbm, bias_hbm, lengths_hbm, dest_hbm, query_hbm, old_hbm, new_hbm, table_hbm,
    out_ref,
    tokens, scaled, weight, gain_ref, bias_ref, lengths_ref, dest_ref, query, old, new_ref, new_keys, new_values, table_ref,
    pair_out, pair_in, own, landing, line_out, final,
    squares, pick, cos_rows, sin_rows, inverse_rms, live, score_old, score_new, outgoing, arrived,
    joined, all_in,
    load_sem, weight_sem, sq_send, sq_recv, pair_send, pair_recv, line_send, line_recv, hand_send, hand_recv,
):
    group = lax.axis_index("grp")
    tp = lax.axis_index("tp")
    chip = tp // 2
    core = tp % 2
    partner = tp + 1 - 2 * core
    plane, layer = group // LAYERS, group % LAYERS

    load_gain = pltpu.make_async_copy(gain_hbm, gain_ref, load_sem.at[0])
    load_tokens = pltpu.make_async_copy(tokens_hbm, tokens, load_sem.at[1])
    load_gain.start()
    load_tokens.start()

    def head_of(step, whose):
        place = jnp.where(chip < 2, CHIPS - 1 - step, step)
        return place, 2 * place + whose

    def load_weight(step, which):
        whose = (1 - core) if which == 0 else core
        _, head = head_of(step, whose)
        columns = pl.ds(pl.multiple_of(head * WIDTH, WIDTH), WIDTH)
        return pltpu.make_async_copy(weight_hbm.at[:, columns], weight.at[4 * which + step], weight_sem.at[4 * which + step])

    for step in range(CHIPS):
        for which in range(2):
            load_weight(step, which).start()
    later_loads = [
        (lengths_hbm, lengths_ref), (dest_hbm, dest_ref), (table_hbm, table_ref), (bias_hbm, bias_ref), (new_hbm, new_ref),
    ]
    for z in range(LAYERS):
        later_loads.append((query_hbm.at[:, z], query.at[z]))
        later_loads.append((old_hbm.at[:, z], old.at[z]))
    later_loads = [
        pltpu.make_async_copy(source, target, load_sem.at[2 + i]) for i, (source, target) in enumerate(later_loads)
    ]
    for load in later_loads:
        load.start()

    barrier = pltpu.get_barrier_semaphore()

    def greet_tp(i, carry):
        peer = (tp + i) % TP

        @pl.when(peer != LEADER)
        def _():
            pl.semaphore_signal(barrier, inc=1, device_id={"tp": peer}, device_id_type=MESH)

        return carry

    def greet_leaders(i, carry):
        pl.semaphore_signal(barrier, inc=1, device_id={"grp": (group + i) % GRP}, device_id_type=MESH)
        return carry

    def tell_group(i, carry):
        pl.semaphore_signal(all_in, inc=1, device_id={"tp": (tp + i) % TP}, device_id_type=MESH)
        return carry

    lax.fori_loop(1, TP, greet_tp, 0)

    @pl.when(tp != LEADER)
    def _():
        pl.semaphore_wait(barrier, TP - 1)
        pl.semaphore_signal(joined, inc=1, device_id={"tp": LEADER}, device_id_type=MESH)

    load_gain.wait()
    load_tokens.wait()
    for h in range(2):
        rows = pl.ds(h * HALF, HALF)
        scaled[rows, :] = (tokens[rows, :].astype(F32) * gain_ref[...][None, :]).astype(BF16)

    def pair_copy(place):
        return pltpu.make_async_remote_copy(
            src_ref=pair_out.at[place], dst_ref=pair_in.at[place],
            send_sem=pair_send.at[place], recv_sem=pair_recv.at[place],
            device_id={"tp": partner}, device_id_type=MESH,
        )

    def line_copy(way, place, h, to):
        rows = pl.ds(h * HALF, HALF)
        return pltpu.make_async_remote_copy(
            src_ref=line_out.at[place, rows], dst_ref=landing.at[way, place, rows],
            send_sem=line_send.at[place, h], recv_sem=line_recv.at[way, place, h],
            device_id={"tp": to}, device_id_type=MESH,
        )

    def block(place, h):
        rows = pl.ds(h * HALF, HALF)
        return own[place, rows] + pair_in[place, rows].astype(F32)

    def multiply_pair(step):
        place, _ = head_of(step, 0)
        load_weight(step, 0).wait()
        pair_out[pl.ds(place, 1)] = dot(scaled[...], weight[step]).astype(BF16)[None]
        if step == 0:
            @pl.when(tp == LEADER)
            def _():
                pl.semaphore_wait(joined, TP - 1)
                lax.fori_loop(1, GRP, greet_leaders, 0)
        pair_copy(place).start()

    def multiply_own(step):
        place, _ = head_of(step, 0)
        load_weight(step, 1).wait()
        own[pl.ds(place, 1)] = dot(scaled[...], weight[4 + step])[None]

    def first_sends(step):
        place, _ = head_of(step, 0)
        way = chip // (CHIPS - 1)

        @pl.when(chip % (CHIPS - 1) == 0)
        def _():
            pair_copy(place).wait_recv()
            for h in range(2):
                rows = pl.ds(h * HALF, HALF)
                line_out[place, rows] = block(place, h).astype(BF16)
                line_copy(way, place, h, tp + 2 - 4 * way).start()

    multiply_pair(0)
    multiply_own(0)
    for step in range(1, CHIPS):
        multiply_pair(step)
        first_sends(step - 1)
        multiply_own(step)

    def square_copy(i):
        return pltpu.make_async_remote_copy(
            src_ref=squares.at[tp], dst_ref=squares.at[tp],
            send_sem=sq_send.at[i], recv_sem=sq_recv.at[tp],
            device_id={"tp": (tp + i) % TP}, device_id_type=MESH,
        )

    def square_arrival(i):
        source = (tp + i) % TP
        return pltpu.make_async_remote_copy(
            src_ref=squares.at[source], dst_ref=squares.at[source],
            send_sem=sq_send.at[i], recv_sem=sq_recv.at[source],
            device_id={"tp": source}, device_id_type=MESH,
        )

    for h in range(2):
        floats = tokens[pl.ds(h * HALF, HALF), :].astype(F32)
        square = floats * floats
        high = square.astype(BF16)
        low = (square - high.astype(F32)).astype(BF16)
        ones = jnp.ones((8, FEATS), BF16)
        sums = dot(ones, high, NT) + dot(ones, low, NT)
        squares[pl.ds(tp, 1), :, h * HALF:(h + 1) * HALF] = sums[0:1, :].reshape(1, 1, HALF)
    for i in range(1, TP):
        square_copy(i).start()

    for load in later_loads:
        load.wait()
    lengths = lengths_ref[...]
    dests = dest_ref[...]
    mine = iota((GRP, GRP), 0) == group
    own_lengths = jnp.sum(jnp.where(mine, lengths, 0), axis=0, keepdims=True)
    own_dest = jnp.sum(jnp.where(mine, dests, 0), axis=0, keepdims=True)
    before = (iota((GRP, GRP), 0) < iota((GRP, GRP), 1)).astype(F32)
    spread = jnp.broadcast_to(own_lengths.astype(F32), (8, GRP))
    starts = dot(spread, before)[0:1, :].astype(jnp.int32)
    by_layer = iota((GRP, GRP), 0) % PLANE * LAYERS + iota((GRP, GRP), 0) // PLANE
    routed = own_dest == by_layer
    slot_first = jnp.sum(jnp.where(routed, starts, 0), axis=1, keepdims=True)
    slot_length = jnp.sum(jnp.where(routed, own_lengths, 0), axis=1, keepdims=True)
    for part in range(8):
        requests = slice(part * 8, part * 8 + 8)
        offset = iota((8, SLOT, ROWS), 1)
        first = slot_first[requests][:, :, None]
        length = slot_length[requests][:, :, None]
        hit = (iota((8, SLOT, ROWS), 2) == first + offset) & (offset < length)
        pick[part // 2, part % 2 * 128:part % 2 * 128 + 128, :] = hit.astype(F32).reshape(128, ROWS).astype(BF16)

    row_index = iota((ROWS, GRP), 0)
    first_row = jnp.max(jnp.where(starts <= row_index, starts, 0), axis=1, keepdims=True)
    at_offset = (iota((ROWS, SLOT), 1) + first_row == iota((ROWS, SLOT), 0)).astype(F32).astype(BF16)
    rest = table_ref[...]
    tabled = jnp.zeros((ROWS, 2 * HD), F32)
    for _ in range(3):
        term = rest.astype(BF16)
        rest = rest - term.astype(F32)
        tabled = tabled + dot(at_offset, term)
    cos_rows[...] = tabled[:, 0:HD]
    sin_rows[...] = tabled[:, HD:2 * HD]

    live_rows = jnp.sum(jnp.where(dests == group, lengths, 0), axis=1, keepdims=True)
    for z in range(LAYERS):
        at_source = iota((GRP, LANES), 1) // SLOT * LAYERS + z == iota((GRP, LANES), 0)
        live_lanes = jnp.sum(jnp.where(at_source, live_rows, 0), axis=0, keepdims=True)
        live[z] = (iota((1, LANES), 1) % SLOT < live_lanes).astype(F32)

    sorted_row = iota((4 * GRP, 4 * GRP), 0)
    natural = (sorted_row // 4 % PLANE * LAYERS + sorted_row // (4 * PLANE)) * 4 + sorted_row % 4
    column = iota((4 * GRP, 4 * GRP), 1)
    new_keys[...] = dot((column == natural).astype(F32).astype(BF16), new_ref[...]).astype(BF16)
    shifted = (column == natural + 2) & (sorted_row % 4 < 2)
    new_values[...] = dot(shifted.astype(F32).astype(BF16), new_ref[...]).astype(BF16)

    scale = 1.0 / math.sqrt(HD)
    same = iota((128, 128), 0) // 16 == iota((128, 128), 1) // 16
    same_new = (iota((128, 32), 0) // 16 == iota((128, 32), 1) // 4) & (iota((128, 32), 1) % 4 <= iota((128, 32), 0) % 2)
    for z in range(LAYERS):
        for half in range(2):
            eight = slice(half * 8, half * 8 + 8)
            asked = query[z, eight].reshape(128, HD)
            cached_keys = old[z, eight, :, 0:HD].reshape(128, HD)
            fresh_keys = new_keys[z * 64 + half * 32:z * 64 + half * 32 + 32, :]
            score_old[2 * z + half] = jnp.where(same, dot(asked, cached_keys, NT) * scale, -1e30)
            score_new[2 * z + half] = jnp.where(same_new, dot(asked, fresh_keys, NT) * scale, -1e30)

    for i in range(1, TP):
        square_arrival(i).wait_recv()
    total = jnp.sum(squares[...].reshape(TP, ROWS), axis=0, keepdims=True)
    inverse_rms[...] = jnp.broadcast_to(lax.rsqrt(total / D + EPSILON), (HD, ROWS)).T

    schedules = {
        0: [(1, 0, 0), (1, 0, 1)],
        1: [(0, 3, 0), (0, 3, 1), (1, 0, 0), (0, 2, 0), (1, 0, 1), (0, 2, 1), (1, 1, 0), (1, 1, 1), (0, 1, 0), (0, 1, 1)],
        2: [(1, 0, 0), (1, 0, 1), (0, 3, 0), (1, 1, 0), (0, 3, 1), (1, 1, 1), (0, 2, 0), (0, 2, 1), (1, 2, 0), (1, 2, 1)],
        3: [(0, 3, 0), (0, 3, 1)],
    }
    for here in range(CHIPS):
        @pl.when(chip == here)
        def _(here=here):
            have = {0: {3, 2, 1}, 3: {0, 1, 2}}.get(here, set())
            begun = set()
            for way, place, h in schedules[here]:
                if place not in have:
                    have.add(place)
                    pair_copy(place).wait_recv()
                rows = pl.ds(h * HALF, HALF)
                value = final[rows, :] if place == here and h in begun else block(place, h)
                line_copy(way, place, h, tp + 4 * way - 2).wait_recv()
                value = value + landing[way, place, rows].astype(F32)
                if place == here:
                    begun.add(h)
                    final[rows, :] = value
                else:
                    line_out[place, rows] = value.astype(BF16)
                    line_copy(way, place, h, tp + 2 - 4 * way).start()

    @pl.when(tp == LEADER)
    def _():
        pl.semaphore_wait(barrier, GRP - 1)
        lax.fori_loop(1, TP, tell_group, 0)

    keys = final[:, 0:HD] * inverse_rms[...] + bias_ref[0:HD][None, :]
    values = final[:, HD:WIDTH] * inverse_rms[...] + bias_ref[HD:WIDTH][None, :]
    turned = pltpu.roll(keys, HD // 2, 1)
    keys = (keys * cos_rows[...] + turned * sin_rows[...]).astype(BF16)
    handed = jnp.concatenate([keys, values.astype(BF16)], axis=1)

    @pl.when(tp != LEADER)
    def _():
        pl.semaphore_wait(all_in, 1)

    y, x = plane // 4, plane % 4

    def send(away, target_layer):
        def body(i, carry):
            target = (y + i // 4) % 4 * 4 + (x + i % 4) % 4
            pltpu.make_async_remote_copy(
                src_ref=outgoing.at[target_layer, target], dst_ref=arrived.at[layer, plane],
                send_sem=hand_send.at[away], recv_sem=hand_recv.at[away],
                device_id={"grp": target * LAYERS + target_layer}, device_id_type=MESH,
            ).start()
            return carry
        return body

    def handed_over(away):
        blocks = pl.ds(0, PLANE if away else PLANE - 1)
        return pltpu.make_async_remote_copy(
            src_ref=outgoing.at[0, blocks], dst_ref=arrived.at[0, blocks],
            send_sem=hand_send.at[away], recv_sem=hand_recv.at[away],
            device_id={"grp": (group + 1) % GRP}, device_id_type=MESH,
        )

    for away in (2, 1, 3, 0):
        target_layer = (layer + away) % LAYERS
        picked = dot(pick[target_layer], handed).astype(BF16)
        outgoing[pl.ds(target_layer, 1)] = picked.reshape(1, PLANE, SLOT, WIDTH)
        lax.fori_loop(0 if away else 1, PLANE, send(away, target_layer), 0)
    arrived[pl.ds(layer, 1), pl.ds(plane, 1)] = outgoing[pl.ds(layer, 1), pl.ds(plane, 1)]

    for away in (0, 1, 3, 2):
        handed_over(away).wait_recv()
        z = (layer + LAYERS - away) % LAYERS
        span_live = live[z] > 0.5
        for half in range(2):
            eight = pl.ds(half * 8, 8)
            asked = query[z, eight].reshape(128, HD)
            old_values = old[z, eight, :, HD:WIDTH].reshape(128, HD)
            span_keys = arrived[z, eight, :, 0:HD].reshape(128, HD)
            span_values = arrived[z, eight, :, HD:WIDTH].reshape(128, HD)
            fresh_values = new_values[pl.ds(pl.multiple_of(z * 64 + half * 32, 32), 32), :]
            cached, fresh = score_old[2 * z + half], score_new[2 * z + half]
            may = same & span_live[:, half * 128:half * 128 + 128]
            span = jnp.where(may, dot(asked, span_keys, NT) * scale, -1e30)
            top = jnp.max(jnp.maximum(cached, span), axis=1, keepdims=True)
            top = jnp.maximum(top, jnp.max(fresh, axis=1, keepdims=True))
            cached, span, fresh = jnp.exp(cached - top), jnp.exp(span - top), jnp.exp(fresh - top)
            weight_sum = jnp.sum(cached + span, axis=1, keepdims=True) + jnp.sum(fresh, axis=1, keepdims=True)
            inverse = 1.0 / weight_sum
            result = dot((cached * inverse).astype(BF16), old_values)
            result = result + dot((span * inverse).astype(BF16), span_values)
            result = result + dot((fresh * inverse).astype(BF16), fresh_values)
            out_ref[eight, pl.ds(z, 1)] = result.astype(BF16).reshape(8, 1, SLOT, HD)

    for place in range(CHIPS):
        pair_copy(place).wait_send()
        for h in range(2):
            @pl.when(chip != place)
            def _(place=place, h=h):
                line_copy(0, place, h, partner).wait_send()
    for i in range(1, TP):
        square_copy(i).wait_send()
    for away in (0, 1, 3, 2):
        handed_over(away).wait_send()


def shards(tokens, gain, kv_weight, kv_bias, lengths, dest, queries, old_cache, new_kv):
    query_rows = queries.reshape(GRP, STEPS, QPK, HD).transpose(0, 2, 1, 3).reshape(PLANE, LAYERS, SLOT, HD)
    new_rows = new_kv.reshape(GRP, STEPS, 2, HD).transpose(0, 2, 1, 3).reshape(4 * GRP, HD)
    any_space = pl.BlockSpec(memory_space=pl.ANY)
    vmem = pl.BlockSpec(memory_space=pltpu.VMEM)
    dma = pltpu.SemaphoreType.DMA
    out = pl.pallas_call(
        kernel,
        out_shape=jax.ShapeDtypeStruct((PLANE, LAYERS, SLOT, HD), BF16),
        in_specs=[any_space] * 10,
        out_specs=vmem,
        scratch_shapes=[
            pltpu.VMEM((ROWS, FEATS), BF16),
            pltpu.VMEM((ROWS, FEATS), BF16),
            pltpu.VMEM((TP, FEATS, WIDTH), BF16),
            pltpu.VMEM((FEATS,), F32),
            pltpu.VMEM((WIDTH,), F32),
            pltpu.VMEM((GRP, GRP), jnp.int32),
            pltpu.VMEM((GRP, GRP), jnp.int32),
            pltpu.VMEM((LAYERS, PLANE, SLOT, HD), BF16),
            pltpu.VMEM((LAYERS, PLANE, SLOT, WIDTH), BF16),
            pltpu.VMEM((4 * GRP, HD), BF16),
            pltpu.VMEM((4 * GRP, HD), BF16),
            pltpu.VMEM((4 * GRP, HD), BF16),
            pltpu.VMEM((SLOT, 2 * HD), F32),
            pltpu.VMEM((CHIPS, ROWS, WIDTH), BF16),
            pltpu.VMEM((CHIPS, ROWS, WIDTH), BF16),
            pltpu.VMEM((CHIPS, ROWS, WIDTH), F32),
            pltpu.VMEM((2, CHIPS, ROWS, WIDTH), BF16),
            pltpu.VMEM((CHIPS, ROWS, WIDTH), BF16),
            pltpu.VMEM((ROWS, WIDTH), F32),
            pltpu.VMEM((TP, 1, ROWS), F32),
            pltpu.VMEM((LAYERS, LANES, ROWS), BF16),
            pltpu.VMEM((ROWS, HD), F32),
            pltpu.VMEM((ROWS, HD), F32),
            pltpu.VMEM((ROWS, HD), F32),
            pltpu.VMEM((LAYERS, 1, LANES), F32),
            pltpu.VMEM((8, 128, 128), F32),
            pltpu.VMEM((8, 128, 32), F32),
            pltpu.VMEM((LAYERS, PLANE, SLOT, WIDTH), BF16),
            pltpu.VMEM((LAYERS, PLANE, SLOT, WIDTH), BF16),
            pltpu.SemaphoreType.REGULAR,
            pltpu.SemaphoreType.REGULAR,
            dma((15,)),
            dma((TP,)),
            dma((TP,)),
            dma((TP,)),
            dma((CHIPS,)),
            dma((CHIPS,)),
            dma((CHIPS, 2)),
            dma((2, CHIPS, 2)),
            dma((LAYERS,)),
            dma((LAYERS,)),
        ],
        compiler_params=pltpu.CompilerParams(
            collective_id=0, has_side_effects=True, vmem_limit_bytes=60 * 1024 * 1024
        ),
        cost_estimate=pl.CostEstimate(flops=2_500_000_000, bytes_accessed=6_000_000, transcendentals=300_000),
    )(
        tokens, kv_weight, gain, kv_bias, lengths, dest,
        query_rows, old_cache.reshape(PLANE, LAYERS, SLOT, WIDTH), new_rows, jnp.asarray(rotary_tables()),
    )
    return out.reshape(GRP, QPK, STEPS, HD).transpose(0, 2, 1, 3).reshape(1, GRP, STEPS, QPK * HD)


def solution(mesh):
    return jax.shard_map(
        shards,
        mesh=mesh,
        in_specs=(
            P("grp", "tp"),
            P("tp"),
            P("tp", None),
            P("tp"),
            P(),
            P(),
            P("grp", None, None, "tp"),
            P("grp", None, None, "tp"),
            P("grp", None, None, "tp"),
        ),
        out_specs=P("grp", None, None, "tp"),
        check_vma=False,
    )
```

time: 74.2 us -> 82.9 us (1.12)
  the two profiles are of different devices: /device:TPU:32 before, /device:TPU:64 now
where the time goes in v3:
time: 82.9 us; the launch traced here: 82.8 us
  Pallas kernels  81 us (98%)
  local copies, waits for them, and re-layouts  1.83 us (2%)
    pallas_call x1, Pallas kernels, shards(): pl.pallas_call(kernel, out_shape=jax.ShapeDtypeStruct((PLANE, LAYERS, SLO...  81 us
    unnamed x1, local copies, waits for them, and re-layouts  1.83 us

profile of v3, /device:TPU:64, one launch (start us, length us, event | category | flops | bytes accessed | tf_op | source)
XLA Modules:
  0.0 82.8 jit_solution(15900022959712954590)
XLA Ops:
  0.0 81.0 %shard_map.100 = bf16[16,4,16,128]{3,2,1,0:T(8,128)(2,1)} custom-call(bf16[512,768]{1,0:T(8,128)(2,1)} %tokens_hbm.1, bf16[768,2048]{1,0:T(8,128)(2,1)} %weight_hbm.1, f32[768]{0:T(1024)} %gain_hbm.1, f32[256]{0:T(256)} %bias_hbm.1, s32[64,64]{1,0:T(8,128)} %lengths_hbm.1, s32[64,64]{1,0:T(8,128)} %dest_hbm.1, bf16[16,4,16,128]{3,2,1,0:T(8,128)(2,1)} %bitcast.18, ...), custom_call_target="tpu_custom_call" | custom-call | flops 2500000000 | bytes 6000000 | tf_op jit(solution)/shard_map/pallas_call | solution.py:390
  81.0 1.8 %copy.15 = bf16[1,64,2,1024]{3,2,1,0:T(2,128)(2,1)} copy(bf16[1,64,2,1024]{3,2,1,0:T(2,128)(2,1)} %bitcast.16) | data formatting | bytes 524288

commit v4 on v3

--- a/solution.py
+++ b/solution.py
@@ -97,8 +97,6 @@
     later_loads = [
         pltpu.make_async_copy(source, target, load_sem.at[2 + i]) for i, (source, target) in enumerate(later_loads)
     ]
-    for load in later_loads:
-        load.start()
 
     barrier = pltpu.get_barrier_semaphore()
 
@@ -179,12 +177,10 @@
                 line_out[place, rows] = block(place, h).astype(BF16)
                 line_copy(way, place, h, tp + 2 - 4 * way).start()
 
-    multiply_pair(0)
-    multiply_own(0)
-    for step in range(1, CHIPS):
+    for load in later_loads:
+        load.start()
+    for step in range(CHIPS):
         multiply_pair(step)
-        first_sends(step - 1)
-        multiply_own(step)
 
     def square_copy(i):
         return pltpu.make_async_remote_copy(
@@ -211,6 +207,11 @@
         squares[pl.ds(tp, 1), :, h * HALF:(h + 1) * HALF] = sums[0:1, :].reshape(1, 1, HALF)
     for i in range(1, TP):
         square_copy(i).start()
+
+    for step in range(CHIPS):
+        multiply_own(step)
+        if step < CHIPS - 1:
+            first_sends(step)
 
     for load in later_loads:
         load.wait()
@@ -270,11 +271,6 @@
             fresh_keys = new_keys[z * 64 + half * 32:z * 64 + half * 32 + 32, :]
             score_old[2 * z + half] = jnp.where(same, dot(asked, cached_keys, NT) * scale, -1e30)
             score_new[2 * z + half] = jnp.where(same_new, dot(asked, fresh_keys, NT) * scale, -1e30)
-
-    for i in range(1, TP):
-        square_arrival(i).wait_recv()
-    total = jnp.sum(squares[...].reshape(TP, ROWS), axis=0, keepdims=True)
-    inverse_rms[...] = jnp.broadcast_to(lax.rsqrt(total / D + EPSILON), (HD, ROWS)).T
 
     schedules = {
         0: [(1, 0, 0), (1, 0, 1)],
@@ -307,6 +303,10 @@
         pl.semaphore_wait(barrier, GRP - 1)
         lax.fori_loop(1, TP, tell_group, 0)
 
+    for i in range(1, TP):
+        square_arrival(i).wait_recv()
+    total = jnp.sum(squares[...].reshape(TP, ROWS), axis=0, keepdims=True)
+    inverse_rms[...] = jnp.broadcast_to(lax.rsqrt(total / D + EPSILON), (HD, ROWS)).T
     keys = final[:, 0:HD] * inverse_rms[...] + bias_ref[0:HD][None, :]
     values = final[:, HD:WIDTH] * inverse_rms[...] + bias_ref[HD:WIDTH][None, :]
     turned = pltpu.roll(keys, HD // 2, 1)
@@ -319,14 +319,20 @@
 
     y, x = plane // 4, plane % 4
 
-    def send(away, target_layer):
+    def send(aways):
         def body(i, carry):
             target = (y + i // 4) % 4 * 4 + (x + i % 4) % 4
-            pltpu.make_async_remote_copy(
-                src_ref=outgoing.at[target_layer, target], dst_ref=arrived.at[layer, plane],
-                send_sem=hand_send.at[away], recv_sem=hand_recv.at[away],
-                device_id={"grp": target * LAYERS + target_layer}, device_id_type=MESH,
-            ).start()
+            for away in aways:
+                target_layer = (layer + away) % LAYERS
+                copy = pltpu.make_async_remote_copy(
+                    src_ref=outgoing.at[target_layer, target], dst_ref=arrived.at[layer, plane],
+                    send_sem=hand_send.at[away], recv_sem=hand_recv.at[away],
+                    device_id={"grp": target * LAYERS + target_layer}, device_id_type=MESH,
+                )
+                if away:
+                    copy.start()
+                else:
+                    pl.when(i > 0)(copy.start)
             return carry
         return body
 
@@ -338,11 +344,12 @@
             device_id={"grp": (group + 1) % GRP}, device_id_type=MESH,
         )
 
-    for away in (2, 1, 3, 0):
-        target_layer = (layer + away) % LAYERS
-        picked = dot(pick[target_layer], handed).astype(BF16)
-        outgoing[pl.ds(target_layer, 1)] = picked.reshape(1, PLANE, SLOT, WIDTH)
-        lax.fori_loop(0 if away else 1, PLANE, send(away, target_layer), 0)
+    for aways in ((1, 3), (2,), (0,)):
+        for away in aways:
+            target_layer = (layer + away) % LAYERS
+            picked = dot(pick[target_layer], handed).astype(BF16)
+            outgoing[pl.ds(target_layer, 1)] = picked.reshape(1, PLANE, SLOT, WIDTH)
+        lax.fori_loop(0, PLANE, send(aways), 0)
     arrived[pl.ds(layer, 1), pl.ds(plane, 1)] = outgoing[pl.ds(layer, 1), pl.ds(plane, 1)]
 
     for away in (0, 1, 3, 2):

time: 82.9 us -> 66.9 us (0.81)
  the two profiles are of different devices: /device:TPU:64 before, /device:TPU:1 now
where the time goes in v4:
time: 66.9 us; the launch traced here: 66.8 us
  Pallas kernels  64.9 us (97%)
  local copies, waits for them, and re-layouts  1.83 us (3%)
    pallas_call x1, Pallas kernels, shards(): pl.pallas_call(kernel, out_shape=jax.ShapeDtypeStruct((PLANE, LAYERS, SLO...  64.9 us
    unnamed x1, local copies, waits for them, and re-layouts  1.83 us

profile of v4, /device:TPU:1, one launch (start us, length us, event | category | flops | bytes accessed | tf_op | source)
XLA Modules:
  0.0 66.8 jit_solution(5065221098969131263)
XLA Ops:
  0.0 64.9 %shard_map.100 = bf16[16,4,16,128]{3,2,1,0:T(8,128)(2,1)} custom-call(bf16[512,768]{1,0:T(8,128)(2,1)} %tokens_hbm.1, bf16[768,2048]{1,0:T(8,128)(2,1)} %weight_hbm.1, f32[768]{0:T(1024)} %gain_hbm.1, f32[256]{0:T(256)} %bias_hbm.1, s32[64,64]{1,0:T(8,128)} %lengths_hbm.1, s32[64,64]{1,0:T(8,128)} %dest_hbm.1, bf16[16,4,16,128]{3,2,1,0:T(8,128)(2,1)} %bitcast.18, ...), custom_call_target="tpu_custom_call" | custom-call | flops 2500000000 | bytes 6000000 | tf_op jit(solution)/shard_map/pallas_call | solution.py:397
  64.9 1.8 %copy.15 = bf16[1,64,2,1024]{3,2,1,0:T(2,128)(2,1)} copy(bf16[1,64,2,1024]{3,2,1,0:T(2,128)(2,1)} %bitcast.16) | data formatting | bytes 524288

commit v5 on v4

--- a/solution.py
+++ b/solution.py
@@ -58,7 +58,7 @@
     tokens_hbm, weight_hbm, gain_hbm, bias_hbm, lengths_hbm, dest_hbm, query_hbm, old_hbm, new_hbm, table_hbm,
     out_ref,
     tokens, scaled, weight, gain_ref, bias_ref, lengths_ref, dest_ref, query, old, new_ref, new_keys, new_values, table_ref,
-    pair_out, pair_in, own, landing, line_out, final,
+    pair_out, pair_in, own, landing, line_out, final, handed,
     squares, pick, cos_rows, sin_rows, inverse_rms, live, score_old, score_new, outgoing, arrived,
     joined, all_in,
     load_sem, weight_sem, sq_send, sq_recv, pair_send, pair_recv, line_send, line_recv, hand_send, hand_recv,
@@ -179,9 +179,6 @@
 
     for load in later_loads:
         load.start()
-    for step in range(CHIPS):
-        multiply_pair(step)
-
     def square_copy(i):
         return pltpu.make_async_remote_copy(
             src_ref=squares.at[tp], dst_ref=squares.at[tp],
@@ -197,6 +194,10 @@
             device_id={"tp": source}, device_id_type=MESH,
         )
 
+    multiply_pair(0)
+    multiply_pair(1)
+    multiply_own(0)
+    first_sends(0)
     for h in range(2):
         floats = tokens[pl.ds(h * HALF, HALF), :].astype(F32)
         square = floats * floats
@@ -207,11 +208,13 @@
         squares[pl.ds(tp, 1), :, h * HALF:(h + 1) * HALF] = sums[0:1, :].reshape(1, 1, HALF)
     for i in range(1, TP):
         square_copy(i).start()
-
-    for step in range(CHIPS):
-        multiply_own(step)
-        if step < CHIPS - 1:
-            first_sends(step)
+    multiply_pair(2)
+    multiply_own(1)
+    first_sends(1)
+    multiply_pair(3)
+    multiply_own(2)
+    first_sends(2)
+    multiply_own(3)
 
     for load in later_loads:
         load.wait()
@@ -278,44 +281,54 @@
         2: [(1, 0, 0), (1, 0, 1), (0, 3, 0), (1, 1, 0), (0, 3, 1), (1, 1, 1), (0, 2, 0), (0, 2, 1), (1, 2, 0), (1, 2, 1)],
         3: [(0, 3, 0), (0, 3, 1)],
     }
-    for here in range(CHIPS):
-        @pl.when(chip == here)
-        def _(here=here):
-            have = {0: {3, 2, 1}, 3: {0, 1, 2}}.get(here, set())
-            begun = set()
-            for way, place, h in schedules[here]:
-                if place not in have:
-                    have.add(place)
-                    pair_copy(place).wait_recv()
-                rows = pl.ds(h * HALF, HALF)
-                value = final[rows, :] if place == here and h in begun else block(place, h)
-                line_copy(way, place, h, tp + 4 * way - 2).wait_recv()
-                value = value + landing[way, place, rows].astype(F32)
-                if place == here:
-                    begun.add(h)
-                    final[rows, :] = value
-                else:
-                    line_out[place, rows] = value.astype(BF16)
-                    line_copy(way, place, h, tp + 2 - 4 * way).start()
+    have = {0: {3, 2, 1}, 1: set(), 2: set(), 3: {0, 1, 2}}
+    begun = {here: set() for here in range(CHIPS)}
+
+    def follow(here, events):
+        for way, place, h in events:
+            if place not in have[here]:
+                have[here].add(place)
+                pair_copy(place).wait_recv()
+            rows = pl.ds(h * HALF, HALF)
+            value = final[rows, :] if place == here and h in begun[here] else block(place, h)
+            line_copy(way, place, h, tp + 4 * way - 2).wait_recv()
+            value = value + landing[way, place, rows].astype(F32)
+            if place == here:
+                begun[here].add(h)
+                final[rows, :] = value
+            else:
+                line_out[place, rows] = value.astype(BF16)
+                line_copy(way, place, h, tp + 2 - 4 * way).start()
+
+    def finish(h):
+        rows = pl.ds(h * HALF, HALF)
+        inverse = inverse_rms[rows, :]
+        keys = final[rows, 0:HD] * inverse + bias_ref[0:HD][None, :]
+        values = final[rows, HD:WIDTH] * inverse + bias_ref[HD:WIDTH][None, :]
+        turned = pltpu.roll(keys, HD // 2, 1)
+        handed[rows, 0:HD] = (keys * cos_rows[rows, :] + turned * sin_rows[rows, :]).astype(BF16)
+        handed[rows, HD:WIDTH] = values.astype(BF16)
 
     @pl.when(tp == LEADER)
     def _():
         pl.semaphore_wait(barrier, GRP - 1)
         lax.fori_loop(1, TP, tell_group, 0)
 
+    for here in range(CHIPS):
+        pl.when(chip == here)(functools.partial(follow, here, schedules[here][:-1]))
     for i in range(1, TP):
         square_arrival(i).wait_recv()
     total = jnp.sum(squares[...].reshape(TP, ROWS), axis=0, keepdims=True)
     inverse_rms[...] = jnp.broadcast_to(lax.rsqrt(total / D + EPSILON), (HD, ROWS)).T
-    keys = final[:, 0:HD] * inverse_rms[...] + bias_ref[0:HD][None, :]
-    values = final[:, HD:WIDTH] * inverse_rms[...] + bias_ref[HD:WIDTH][None, :]
-    turned = pltpu.roll(keys, HD // 2, 1)
-    keys = (keys * cos_rows[...] + turned * sin_rows[...]).astype(BF16)
-    handed = jnp.concatenate([keys, values.astype(BF16)], axis=1)
+    finish(0)
 
     @pl.when(tp != LEADER)
     def _():
         pl.semaphore_wait(all_in, 1)
+
+    for here in range(CHIPS):
+        pl.when(chip == here)(functools.partial(follow, here, schedules[here][-1:]))
+    finish(1)
 
     y, x = plane // 4, plane % 4
 
@@ -347,7 +360,7 @@
     for aways in ((1, 3), (2,), (0,)):
         for away in aways:
             target_layer = (layer + away) % LAYERS
-            picked = dot(pick[target_layer], handed).astype(BF16)
+            picked = dot(pick[target_layer], handed[...]).astype(BF16)
             outgoing[pl.ds(target_layer, 1)] = picked.reshape(1, PLANE, SLOT, WIDTH)
         lax.fori_loop(0, PLANE, send(aways), 0)
     arrived[pl.ds(layer, 1), pl.ds(plane, 1)] = outgoing[pl.ds(layer, 1), pl.ds(plane, 1)]
@@ -391,13 +404,12 @@
 def shards(tokens, gain, kv_weight, kv_bias, lengths, dest, queries, old_cache, new_kv):
     query_rows = queries.reshape(GRP, STEPS, QPK, HD).transpose(0, 2, 1, 3).reshape(PLANE, LAYERS, SLOT, HD)
     new_rows = new_kv.reshape(GRP, STEPS, 2, HD).transpose(0, 2, 1, 3).reshape(4 * GRP, HD)
-    any_space = pl.BlockSpec(memory_space=pl.ANY)
     vmem = pl.BlockSpec(memory_space=pltpu.VMEM)
     dma = pltpu.SemaphoreType.DMA
     out = pl.pallas_call(
         kernel,
         out_shape=jax.ShapeDtypeStruct((PLANE, LAYERS, SLOT, HD), BF16),
-        in_specs=[any_space] * 10,
+        in_specs=[pl.BlockSpec(memory_space=pltpu.HBM)] * 10,
         out_specs=vmem,
         scratch_shapes=[
             pltpu.VMEM((ROWS, FEATS), BF16),
@@ -419,6 +431,7 @@
             pltpu.VMEM((2, CHIPS, ROWS, WIDTH), BF16),
             pltpu.VMEM((CHIPS, ROWS, WIDTH), BF16),
             pltpu.VMEM((ROWS, WIDTH), F32),
+            pltpu.VMEM((ROWS, WIDTH), BF16),
             pltpu.VMEM((TP, 1, ROWS), F32),
             pltpu.VMEM((LAYERS, LANES, ROWS), BF16),
             pltpu.VMEM((ROWS, HD), F32),
@@ -443,12 +456,17 @@
             dma((LAYERS,)),
         ],
         compiler_params=pltpu.CompilerParams(
-            collective_id=0, has_side_effects=True, vmem_limit_bytes=60 * 1024 * 1024
+            collective_id=0, has_side_effects=True, vmem_limit_bytes=40 * 1024 * 1024
         ),
         cost_estimate=pl.CostEstimate(flops=2_500_000_000, bytes_accessed=6_000_000, transcendentals=300_000),
     )(
-        tokens, kv_weight, gain, kv_bias, lengths, dest,
-        query_rows, old_cache.reshape(PLANE, LAYERS, SLOT, WIDTH), new_rows, jnp.asarray(rotary_tables()),
+        *(
+            pltpu.with_memory_space_constraint(operand, pltpu.HBM)
+            for operand in (
+                tokens, kv_weight, gain, kv_bias, lengths, dest,
+                query_rows, old_cache.reshape(PLANE, LAYERS, SLOT, WIDTH), new_rows, jnp.asarray(rotary_tables()),
+            )
+        )
     )
     return out.reshape(GRP, QPK, STEPS, HD).transpose(0, 2, 1, 3).reshape(1, GRP, STEPS, QPK * HD)
 

time: 66.9 us -> 63 us (0.942)
  the two profiles are of different devices: /device:TPU:1 before, /device:TPU:32 now
where the time goes in v5:
time: 63 us; the launch traced here: 62.9 us
  Pallas kernels  62.2 us (99%)
  local copies, waits for them, and re-layouts  0.71 us (1%)
    pallas_call x1, Pallas kernels, shards(): pl.pallas_call(kernel, out_shape=jax.ShapeDtypeStruct((PLANE, LAYERS, SLO...  62.2 us

profile of v5, /device:TPU:32, one launch (start us, length us, event | category | flops | bytes accessed | tf_op | source)
XLA Modules:
  0.0 62.9 jit_solution(17418232923476801045)
XLA Ops:
  0.0 62.2 %shard_map.100 = bf16[16,4,16,128]{3,2,1,0:T(8,128)(2,1)S(1)} custom-call(bf16[512,768]{1,0:T(8,128)(2,1)} %tokens_hbm.1, bf16[768,2048]{1,0:T(8,128)(2,1)} %weight_hbm.1, f32[768]{0:T(1024)} %gain_hbm.1, f32[256]{0:T(256)} %bias_hbm.1, s32[64,64]{1,0:T(8,128)} %lengths_hbm.1, s32[64,64]{1,0:T(8,128)} %dest_hbm.1, bf16[16,4,16,128]{3,2,1,0:T(8,128)(2,1)} %bitcast.18, ...), custom_call_target="tpu_custom_call" | custom-call | flops 2500000000 | bytes 6000000 | tf_op jit(solution)/shard_map/pallas_call | solution.py:409
  62.2 0.7 %copy.15 = bf16[1,64,2,1024]{3,2,1,0:T(2,128)(2,1)} copy(bf16[1,64,2,1024]{3,2,1,0:T(2,128)(2,1)S(1)} %bitcast.16) | data formatting | bytes 524288

commit v6 on v5

--- a/solution.py
+++ b/solution.py
@@ -31,6 +31,10 @@
 PLANE = GRP // LAYERS
 LANES = PLANE * SLOT
 LEADER = 7
+CHUNKS = 4
+PIECES = 2
+LAG = 0.4
+PIECE = ROWS // PIECES
 MESH = pl.DeviceIdType.MESH
 F32 = jnp.float32
 BF16 = jnp.bfloat16
@@ -79,15 +83,15 @@
         place = jnp.where(chip < 2, CHIPS - 1 - step, step)
         return place, 2 * place + whose
 
-    def load_weight(step, which):
-        whose = (1 - core) if which == 0 else core
-        _, head = head_of(step, whose)
-        columns = pl.ds(pl.multiple_of(head * WIDTH, WIDTH), WIDTH)
-        return pltpu.make_async_copy(weight_hbm.at[:, columns], weight.at[4 * which + step], weight_sem.at[4 * which + step])
-
-    for step in range(CHIPS):
-        for which in range(2):
-            load_weight(step, which).start()
+    def load_weight(chunk):
+        rows = pl.ds(chunk * (FEATS // CHUNKS), FEATS // CHUNKS)
+        return pltpu.make_async_copy(weight_hbm.at[rows], weight.at[rows], weight_sem.at[chunk])
+
+    def head_weight(head):
+        return weight[:, pl.ds(pl.multiple_of(head * WIDTH, WIDTH), WIDTH)]
+
+    for chunk in range(CHUNKS):
+        load_weight(chunk).start()
     later_loads = [
         (lengths_hbm, lengths_ref), (dest_hbm, dest_ref), (table_hbm, table_ref), (bias_hbm, bias_ref), (new_hbm, new_ref),
     ]
@@ -119,16 +123,16 @@
 
     lax.fori_loop(1, TP, greet_tp, 0)
 
-    @pl.when(tp != LEADER)
-    def _():
-        pl.semaphore_wait(barrier, TP - 1)
-        pl.semaphore_signal(joined, inc=1, device_id={"tp": LEADER}, device_id_type=MESH)
-
     load_gain.wait()
     load_tokens.wait()
     for h in range(2):
         rows = pl.ds(h * HALF, HALF)
         scaled[rows, :] = (tokens[rows, :].astype(F32) * gain_ref[...][None, :]).astype(BF16)
+
+    @pl.when(tp != LEADER)
+    def _():
+        pl.semaphore_wait(barrier, TP - 1)
+        pl.semaphore_signal(joined, inc=1, device_id={"tp": LEADER}, device_id_type=MESH)
 
     def pair_copy(place):
         return pltpu.make_async_remote_copy(
@@ -138,7 +142,7 @@
         )
 
     def line_copy(way, place, h, to):
-        rows = pl.ds(h * HALF, HALF)
+        rows = pl.ds(h * PIECE, PIECE)
         return pltpu.make_async_remote_copy(
             src_ref=line_out.at[place, rows], dst_ref=landing.at[way, place, rows],
             send_sem=line_send.at[place, h], recv_sem=line_recv.at[way, place, h],
@@ -146,13 +150,12 @@
         )
 
     def block(place, h):
-        rows = pl.ds(h * HALF, HALF)
+        rows = pl.ds(h * PIECE, PIECE)
         return own[place, rows] + pair_in[place, rows].astype(F32)
 
     def multiply_pair(step):
-        place, _ = head_of(step, 0)
-        load_weight(step, 0).wait()
-        pair_out[pl.ds(place, 1)] = dot(scaled[...], weight[step]).astype(BF16)[None]
+        place, head = head_of(step, 1 - core)
+        pair_out[pl.ds(place, 1)] = dot(scaled[...], head_weight(head)).astype(BF16)[None]
         if step == 0:
             @pl.when(tp == LEADER)
             def _():
@@ -161,9 +164,8 @@
         pair_copy(place).start()
 
     def multiply_own(step):
-        place, _ = head_of(step, 0)
-        load_weight(step, 1).wait()
-        own[pl.ds(place, 1)] = dot(scaled[...], weight[4 + step])[None]
+        place, head = head_of(step, core)
+        own[pl.ds(place, 1)] = dot(scaled[...], head_weight(head))[None]
 
     def first_sends(step):
         place, _ = head_of(step, 0)
@@ -172,13 +174,14 @@
         @pl.when(chip % (CHIPS - 1) == 0)
         def _():
             pair_copy(place).wait_recv()
-            for h in range(2):
-                rows = pl.ds(h * HALF, HALF)
+            for h in range(PIECES):
+                rows = pl.ds(h * PIECE, PIECE)
                 line_out[place, rows] = block(place, h).astype(BF16)
                 line_copy(way, place, h, tp + 2 - 4 * way).start()
 
     for load in later_loads:
         load.start()
+
     def square_copy(i):
         return pltpu.make_async_remote_copy(
             src_ref=squares.at[tp], dst_ref=squares.at[tp],
@@ -194,10 +197,12 @@
             device_id={"tp": source}, device_id_type=MESH,
         )
 
+    for chunk in range(CHUNKS):
+        load_weight(chunk).wait()
     multiply_pair(0)
-    multiply_pair(1)
     multiply_own(0)
     first_sends(0)
+    multiply_pair(1)
     for h in range(2):
         floats = tokens[pl.ds(h * HALF, HALF), :].astype(F32)
         square = floats * floats
@@ -275,12 +280,19 @@
             score_old[2 * z + half] = jnp.where(same, dot(asked, cached_keys, NT) * scale, -1e30)
             score_new[2 * z + half] = jnp.where(same_new, dot(asked, fresh_keys, NT) * scale, -1e30)
 
-    schedules = {
-        0: [(1, 0, 0), (1, 0, 1)],
-        1: [(0, 3, 0), (0, 3, 1), (1, 0, 0), (0, 2, 0), (1, 0, 1), (0, 2, 1), (1, 1, 0), (1, 1, 1), (0, 1, 0), (0, 1, 1)],
-        2: [(1, 0, 0), (1, 0, 1), (0, 3, 0), (1, 1, 0), (0, 3, 1), (1, 1, 1), (0, 2, 0), (0, 2, 1), (1, 2, 0), (1, 2, 1)],
-        3: [(0, 3, 0), (0, 3, 1)],
-    }
+    def schedule(here):
+        events = []
+        for way in range(2):
+            from_end = here if way == 0 else CHIPS - 1 - here
+            for back in range(CHIPS - 1):
+                place = CHIPS - 1 - back if way == 0 else back
+                if from_end and (place >= here if way == 0 else place <= here):
+                    for h in range(PIECES):
+                        sent = back * PIECES + h + 1
+                        events.append((sent + from_end * LAG + (from_end - 1), way, place, h))
+        return [event[1:] for event in sorted(events)]
+
+    schedules = {here: schedule(here) for here in range(CHIPS)}
     have = {0: {3, 2, 1}, 1: set(), 2: set(), 3: {0, 1, 2}}
     begun = {here: set() for here in range(CHIPS)}
 
@@ -289,7 +301,7 @@
             if place not in have[here]:
                 have[here].add(place)
                 pair_copy(place).wait_recv()
-            rows = pl.ds(h * HALF, HALF)
+            rows = pl.ds(h * PIECE, PIECE)
             value = final[rows, :] if place == here and h in begun[here] else block(place, h)
             line_copy(way, place, h, tp + 4 * way - 2).wait_recv()
             value = value + landing[way, place, rows].astype(F32)
@@ -300,8 +312,7 @@
                 line_out[place, rows] = value.astype(BF16)
                 line_copy(way, place, h, tp + 2 - 4 * way).start()
 
-    def finish(h):
-        rows = pl.ds(h * HALF, HALF)
+    def finish(rows):
         inverse = inverse_rms[rows, :]
         keys = final[rows, 0:HD] * inverse + bias_ref[0:HD][None, :]
         values = final[rows, HD:WIDTH] * inverse + bias_ref[HD:WIDTH][None, :]
@@ -320,7 +331,7 @@
         square_arrival(i).wait_recv()
     total = jnp.sum(squares[...].reshape(TP, ROWS), axis=0, keepdims=True)
     inverse_rms[...] = jnp.broadcast_to(lax.rsqrt(total / D + EPSILON), (HD, ROWS)).T
-    finish(0)
+    finish(pl.ds(0, ROWS - PIECE))
 
     @pl.when(tp != LEADER)
     def _():
@@ -328,7 +339,7 @@
 
     for here in range(CHIPS):
         pl.when(chip == here)(functools.partial(follow, here, schedules[here][-1:]))
-    finish(1)
+    finish(pl.ds(ROWS - PIECE, PIECE))
 
     y, x = plane // 4, plane % 4
 
@@ -391,7 +402,7 @@
 
     for place in range(CHIPS):
         pair_copy(place).wait_send()
-        for h in range(2):
+        for h in range(PIECES):
             @pl.when(chip != place)
             def _(place=place, h=h):
                 line_copy(0, place, h, partner).wait_send()
@@ -414,7 +425,7 @@
         scratch_shapes=[
             pltpu.VMEM((ROWS, FEATS), BF16),
             pltpu.VMEM((ROWS, FEATS), BF16),
-            pltpu.VMEM((TP, FEATS, WIDTH), BF16),
+            pltpu.VMEM((FEATS, KVW), BF16),
             pltpu.VMEM((FEATS,), F32),
             pltpu.VMEM((WIDTH,), F32),
             pltpu.VMEM((GRP, GRP), jnp.int32),
@@ -445,13 +456,13 @@
             pltpu.SemaphoreType.REGULAR,
             pltpu.SemaphoreType.REGULAR,
             dma((15,)),
-            dma((TP,)),
+            dma((CHUNKS,)),
             dma((TP,)),
             dma((TP,)),
             dma((CHIPS,)),
             dma((CHIPS,)),
-            dma((CHIPS, 2)),
-            dma((2, CHIPS, 2)),
+            dma((CHIPS, PIECES)),
+            dma((2, CHIPS, PIECES)),
             dma((LAYERS,)),
             dma((LAYERS,)),
         ],

time: 63 us -> 62.4 us (level)
  no operation moved by 1% of the time
where the time goes in v6:
time: 62.4 us; the launch traced here: 62.3 us
  Pallas kernels  61.6 us (99%)
  local copies, waits for them, and re-layouts  0.71 us (1%)
    pallas_call x1, Pallas kernels, shards(): pl.pallas_call(kernel, out_shape=jax.ShapeDtypeStruct((PLANE, LAYERS, SLO...  61.6 us

profile of v6, /device:TPU:32, one launch (start us, length us, event | category | flops | bytes accessed | tf_op | source)
XLA Modules:
  0.0 62.3 jit_solution(8562637575795483781)
XLA Ops:
  0.0 61.6 %shard_map.100 = bf16[16,4,16,128]{3,2,1,0:T(8,128)(2,1)S(1)} custom-call(bf16[512,768]{1,0:T(8,128)(2,1)} %tokens_hbm.1, bf16[768,2048]{1,0:T(8,128)(2,1)} %weight_hbm.1, f32[768]{0:T(1024)} %gain_hbm.1, f32[256]{0:T(256)} %bias_hbm.1, s32[64,64]{1,0:T(8,128)} %lengths_hbm.1, s32[64,64]{1,0:T(8,128)} %dest_hbm.1, bf16[16,4,16,128]{3,2,1,0:T(8,128)(2,1)} %bitcast.18, ...), custom_call_target="tpu_custom_call" | custom-call | flops 2500000000 | bytes 6000000 | tf_op jit(solution)/shard_map/pallas_call | solution.py:420
  61.6 0.7 %copy.15 = bf16[1,64,2,1024]{3,2,1,0:T(2,128)(2,1)} copy(bf16[1,64,2,1024]{3,2,1,0:T(2,128)(2,1)S(1)} %bitcast.16) | data formatting | bytes 524288

commit v7 on v6

--- a/solution.py
+++ b/solution.py
@@ -31,7 +31,7 @@
 PLANE = GRP // LAYERS
 LANES = PLANE * SLOT
 LEADER = 7
-CHUNKS = 4
+CHUNKS = 3
 PIECES = 2
 LAG = 0.4
 PIECE = ROWS // PIECES
@@ -62,7 +62,7 @@
     tokens_hbm, weight_hbm, gain_hbm, bias_hbm, lengths_hbm, dest_hbm, query_hbm, old_hbm, new_hbm, table_hbm,
     out_ref,
     tokens, scaled, weight, gain_ref, bias_ref, lengths_ref, dest_ref, query, old, new_ref, new_keys, new_values, table_ref,
-    pair_out, pair_in, own, landing, line_out, final, handed,
+    pair_out, pair_in, own, landing, line_out, final, handed, early,
     squares, pick, cos_rows, sin_rows, inverse_rms, live, score_old, score_new, outgoing, arrived,
     joined, all_in,
     load_sem, weight_sem, sq_send, sq_recv, pair_send, pair_recv, line_send, line_recv, hand_send, hand_recv,
@@ -156,12 +156,34 @@
     def multiply_pair(step):
         place, head = head_of(step, 1 - core)
         pair_out[pl.ds(place, 1)] = dot(scaled[...], head_weight(head)).astype(BF16)[None]
-        if step == 0:
-            @pl.when(tp == LEADER)
-            def _():
-                pl.semaphore_wait(joined, TP - 1)
-                lax.fori_loop(1, GRP, greet_leaders, 0)
         pair_copy(place).start()
+
+    def multiply_first():
+        place, pair_head = head_of(0, 1 - core)
+        _, own_head = head_of(0, core)
+        depth = FEATS // CHUNKS
+        for chunk in range(CHUNKS):
+            load_weight(chunk).wait()
+            features = slice(chunk * depth, chunk * depth + depth)
+            part = scaled[:, features]
+            pair_part = dot(part, weight[features, pl.ds(pl.multiple_of(pair_head * WIDTH, WIDTH), WIDTH)])
+            own_part = dot(part, weight[features, pl.ds(pl.multiple_of(own_head * WIDTH, WIDTH), WIDTH)])
+            if chunk == 0:
+                final[...] = pair_part
+                own[pl.ds(place, 1)] = own_part[None]
+            elif chunk < CHUNKS - 1:
+                final[...] += pair_part
+                own[pl.ds(place, 1)] += own_part[None]
+            else:
+                pair_out[pl.ds(place, 1)] = (final[...] + pair_part).astype(BF16)[None]
+
+                @pl.when(tp == LEADER)
+                def _():
+                    pl.semaphore_wait(joined, TP - 1)
+                    lax.fori_loop(1, GRP, greet_leaders, 0)
+
+                pair_copy(place).start()
+                own[pl.ds(place, 1)] += own_part[None]
 
     def multiply_own(step):
         place, head = head_of(step, core)
@@ -197,10 +219,7 @@
             device_id={"tp": source}, device_id_type=MESH,
         )
 
-    for chunk in range(CHUNKS):
-        load_weight(chunk).wait()
-    multiply_pair(0)
-    multiply_own(0)
+    multiply_first()
     first_sends(0)
     multiply_pair(1)
     for h in range(2):
@@ -332,6 +351,8 @@
     total = jnp.sum(squares[...].reshape(TP, ROWS), axis=0, keepdims=True)
     inverse_rms[...] = jnp.broadcast_to(lax.rsqrt(total / D + EPSILON), (HD, ROWS)).T
     finish(pl.ds(0, ROWS - PIECE))
+    for z in range(LAYERS):
+        early[z] = dot(pick[z, :, 0:ROWS - PIECE], handed[0:ROWS - PIECE, :])
 
     @pl.when(tp != LEADER)
     def _():
@@ -371,7 +392,8 @@
     for aways in ((1, 3), (2,), (0,)):
         for away in aways:
             target_layer = (layer + away) % LAYERS
-            picked = dot(pick[target_layer], handed[...]).astype(BF16)
+            late = dot(pick[target_layer, :, ROWS - PIECE:ROWS], handed[ROWS - PIECE:ROWS, :])
+            picked = (early[target_layer] + late).astype(BF16)
             outgoing[pl.ds(target_layer, 1)] = picked.reshape(1, PLANE, SLOT, WIDTH)
         lax.fori_loop(0, PLANE, send(aways), 0)
     arrived[pl.ds(layer, 1), pl.ds(plane, 1)] = outgoing[pl.ds(layer, 1), pl.ds(plane, 1)]
@@ -443,6 +465,7 @@
             pltpu.VMEM((CHIPS, ROWS, WIDTH), BF16),
             pltpu.VMEM((ROWS, WIDTH), F32),
             pltpu.VMEM((ROWS, WIDTH), BF16),
+            pltpu.VMEM((LAYERS, LANES, WIDTH), F32),
             pltpu.VMEM((TP, 1, ROWS), F32),
             pltpu.VMEM((LAYERS, LANES, ROWS), BF16),
             pltpu.VMEM((ROWS, HD), F32),

time: 62.4 us -> 63.6 us (1.019)
  the two profiles are of different devices: /device:TPU:32 before, /device:TPU:64 now
where the time goes in v7:
time: 63.6 us; the launch traced here: 63.5 us
  Pallas kernels  62.7 us (99%)
  local copies, waits for them, and re-layouts  0.71 us (1%)
    pallas_call x1, Pallas kernels, shards(): pl.pallas_call(kernel, out_shape=jax.ShapeDtypeStruct((PLANE, LAYERS, SLO...  62.7 us

profile of v7, /device:TPU:64, one launch (start us, length us, event | category | flops | bytes accessed | tf_op | source)
XLA Modules:
  0.0 63.5 jit_solution(292728824527745641)
XLA Ops:
  0.0 62.7 %shard_map.100 = bf16[16,4,16,128]{3,2,1,0:T(8,128)(2,1)S(1)} custom-call(bf16[512,768]{1,0:T(8,128)(2,1)} %tokens_hbm.1, bf16[768,2048]{1,0:T(8,128)(2,1)} %weight_hbm.1, f32[768]{0:T(1024)} %gain_hbm.1, f32[256]{0:T(256)} %bias_hbm.1, s32[64,64]{1,0:T(8,128)} %lengths_hbm.1, s32[64,64]{1,0:T(8,128)} %dest_hbm.1, bf16[16,4,16,128]{3,2,1,0:T(8,128)(2,1)} %bitcast.18, ...), custom_call_target="tpu_custom_call" | custom-call | flops 2500000000 | bytes 6000000 | tf_op jit(solution)/shard_map/pallas_call | solution.py:442
  62.8 0.7 %copy.15 = bf16[1,64,2,1024]{3,2,1,0:T(2,128)(2,1)} copy(bf16[1,64,2,1024]{3,2,1,0:T(2,128)(2,1)S(1)} %bitcast.16) | data formatting | bytes 524288

commit v8 on v6

--- a/solution.py
+++ b/solution.py
@@ -62,7 +62,7 @@
     tokens_hbm, weight_hbm, gain_hbm, bias_hbm, lengths_hbm, dest_hbm, query_hbm, old_hbm, new_hbm, table_hbm,
     out_ref,
     tokens, scaled, weight, gain_ref, bias_ref, lengths_ref, dest_ref, query, old, new_ref, new_keys, new_values, table_ref,
-    pair_out, pair_in, own, landing, line_out, final, handed,
+    pair_out, pair_in, own, landing, line_out, final, handed, early,
     squares, pick, cos_rows, sin_rows, inverse_rms, live, score_old, score_new, outgoing, arrived,
     joined, all_in,
     load_sem, weight_sem, sq_send, sq_recv, pair_send, pair_recv, line_send, line_recv, hand_send, hand_recv,
@@ -332,6 +332,8 @@
     total = jnp.sum(squares[...].reshape(TP, ROWS), axis=0, keepdims=True)
     inverse_rms[...] = jnp.broadcast_to(lax.rsqrt(total / D + EPSILON), (HD, ROWS)).T
     finish(pl.ds(0, ROWS - PIECE))
+    for z in range(LAYERS):
+        early[z] = dot(pick[z, :, 0:ROWS - PIECE], handed[0:ROWS - PIECE, :])
 
     @pl.when(tp != LEADER)
     def _():
@@ -371,7 +373,8 @@
     for aways in ((1, 3), (2,), (0,)):
         for away in aways:
             target_layer = (layer + away) % LAYERS
-            picked = dot(pick[target_layer], handed[...]).astype(BF16)
+            late = dot(pick[target_layer, :, ROWS - PIECE:ROWS], handed[ROWS - PIECE:ROWS, :])
+            picked = (early[target_layer] + late).astype(BF16)
             outgoing[pl.ds(target_layer, 1)] = picked.reshape(1, PLANE, SLOT, WIDTH)
         lax.fori_loop(0, PLANE, send(aways), 0)
     arrived[pl.ds(layer, 1), pl.ds(plane, 1)] = outgoing[pl.ds(layer, 1), pl.ds(plane, 1)]
@@ -443,6 +446,7 @@
             pltpu.VMEM((CHIPS, ROWS, WIDTH), BF16),
             pltpu.VMEM((ROWS, WIDTH), F32),
             pltpu.VMEM((ROWS, WIDTH), BF16),
+            pltpu.VMEM((LAYERS, LANES, WIDTH), F32),
             pltpu.VMEM((TP, 1, ROWS), F32),
             pltpu.VMEM((LAYERS, LANES, ROWS), BF16),
             pltpu.VMEM((ROWS, HD), F32),

time: 62.4 us -> 62.4 us (level)
  no operation moved by 1% of the time
where the time goes in v8:
time: 62.4 us; the launch traced here: 62.3 us
  Pallas kernels  61.6 us (99%)
  local copies, waits for them, and re-layouts  0.71 us (1%)
    pallas_call x1, Pallas kernels, shards(): pl.pallas_call(kernel, out_shape=jax.ShapeDtypeStruct((PLANE, LAYERS, SLO...  61.6 us

profile of v8, /device:TPU:32, one launch (start us, length us, event | category | flops | bytes accessed | tf_op | source)
XLA Modules:
  0.0 62.3 jit_solution(15883384128867294423)
XLA Ops:
  0.0 61.6 %shard_map.100 = bf16[16,4,16,128]{3,2,1,0:T(8,128)(2,1)S(1)} custom-call(bf16[512,768]{1,0:T(8,128)(2,1)} %tokens_hbm.1, bf16[768,2048]{1,0:T(8,128)(2,1)} %weight_hbm.1, f32[768]{0:T(1024)} %gain_hbm.1, f32[256]{0:T(256)} %bias_hbm.1, s32[64,64]{1,0:T(8,128)} %lengths_hbm.1, s32[64,64]{1,0:T(8,128)} %dest_hbm.1, bf16[16,4,16,128]{3,2,1,0:T(8,128)(2,1)} %bitcast.18, ...), custom_call_target="tpu_custom_call" | custom-call | flops 2500000000 | bytes 6000000 | tf_op jit(solution)/shard_map/pallas_call | solution.py:423
  61.6 0.7 %copy.15 = bf16[1,64,2,1024]{3,2,1,0:T(2,128)(2,1)} copy(bf16[1,64,2,1024]{3,2,1,0:T(2,128)(2,1)S(1)} %bitcast.16) | data formatting | bytes 524288
